TPU v7x, 32 devices: a whole 2x2x4 slice. The times are simulated.
32 devices in a mesh: dp: 8 (over y, x, core), seq: 4 (over z).
Axes of the slice: x: 2, y: 2, z: 4, core: 2. Of those that a mesh axis runs over, the one named last changes fastest.
Arguments:
- hidden_in: bfloat16 [8, 512, 1024], P('dp', 'seq'), may hold values from -6 to 6
- out_grad: bfloat16 [8, 512, 1024], P('dp', 'seq'), may hold values from -6 to 6
- norm_params: bfloat16 [4096], P(('dp', 'seq')), may hold values from -1 to 1.625
- biases: bfloat16 [8192], P(('dp', 'seq')), may hold values from -1.796875 to 1.796875
- attn_in: bfloat16 [1024, 3072], P('dp', 'seq'), may hold values from -0.1875 to 0.1875
- attn_out: bfloat16 [1024, 1024], P('seq', 'dp'), may hold values from -1 to 1
- mlp_up: bfloat16 [1024, 4096], P('dp', 'seq'), may hold values from -0.1875 to 0.1875
- mlp_down: bfloat16 [4096, 1024], P('seq', 'dp'), may hold values from -0.09375 to 0.09375
Outputs:
- layer_out: bfloat16 [8, 512, 1024], P('dp', 'seq')
- grad_input: bfloat16 [8, 512, 1024], P('dp', 'seq')
- grad_norm: float32 [4096], P(('dp', 'seq'))
- grad_bias: float32 [8192], P(('dp', 'seq'))
- grad_attn_in: float32 [1024, 3072], P('dp', 'seq')
- grad_attn_out: float32 [1024, 1024], P('seq', 'dp')
- grad_up: float32 [1024, 4096], P('dp', 'seq')
- grad_down: float32 [4096, 1024], P('seq', 'dp')
All inputs are finite; a program needn't handle non-finite values.
Results may differ from a plain program's by a relative error of at most 0.011.
Values may be sent and summed in bfloat16 or wider, within the bound.
A program may use at most 40 MiB of HBM per device.

v0:
```python
import math

import jax
import jax.numpy as jnp
from jax import lax
from jax.sharding import PartitionSpec as P

D = 1024
H = 16
HD = 64
FF = 4096
ROT = 16


norm_eps = 1e-05
masked_score = -1e30


def rotary_tables(positions):
    half_rot = ROT // 2
    frequency = jnp.power(
        jnp.float32(10000.0), -2.0 * jnp.arange(half_rot, dtype=jnp.float32) / ROT
    )
    angles = positions[:, None] * frequency[None, :]
    return (jnp.cos(angles)[:, None, :], jnp.sin(angles)[:, None, :])


def rotate(tensor, cosine_table, sine_table):
    half_rot = ROT // 2
    first_half = tensor[..., :half_rot]
    second = tensor[..., half_rot:ROT]
    untouched = tensor[..., ROT:]
    return jnp.concatenate(
        [
            first_half * cosine_table - second * sine_table,
            second * cosine_table + first_half * sine_table,
            untouched,
        ],
        axis=-1,
    )


def rotate_back(tensor, cosine_table, sine_table):
    half_rot = ROT // 2
    first_half = tensor[..., :half_rot]
    second = tensor[..., half_rot:ROT]
    untouched = tensor[..., ROT:]
    return jnp.concatenate(
        [
            first_half * cosine_table + second * sine_table,
            second * cosine_table - first_half * sine_table,
            untouched,
        ],
        axis=-1,
    )


def gelu(values):
    return 0.5 * values * (1.0 + jax.scipy.special.erf(values * (1.0 / math.sqrt(2.0))))


def gelu_slope(values):
    return 0.5 * (1.0 + jax.scipy.special.erf(values * (1.0 / math.sqrt(2.0)))) + values * jnp.exp(
        -0.5 * values * values
    ) * (1.0 / math.sqrt(2.0 * math.pi))


def score_block(queries, keys_full, causal):
    raw_scores = jnp.einsum(
        "sqhe,skhe->shqk", queries, keys_full, preferred_element_type=jnp.float32
    ) * HD ** (-0.5)
    return jnp.where(causal, raw_scores, masked_score)


def attend_forward(queries, keys_full, values_full, causal):
    scores = score_block(queries, keys_full, causal)
    row_max = jnp.max(scores, axis=-1, keepdims=True)
    log_total = row_max + jnp.log(jnp.sum(jnp.exp(scores - row_max), axis=-1, keepdims=True))
    probs_low = jnp.exp(scores - log_total).astype(jnp.bfloat16)
    mixed_heads = jnp.einsum(
        "shqk,skhe->sqhe", probs_low, values_full, preferred_element_type=jnp.float32
    )
    return (mixed_heads, log_total)


def attend_backward(queries, keys_full, values_full, causal, log_total, mixed_heads):
    scores = score_block(queries, keys_full, causal)
    attn_probs = jnp.exp(scores - log_total)
    probs_low = attn_probs.astype(jnp.bfloat16)
    probs_grad = jnp.einsum(
        "sqhe,skhe->shqk", mixed_heads, values_full, preferred_element_type=jnp.float32
    )
    value_term = jnp.einsum(
        "shqk,sqhe->skhe", probs_low, mixed_heads, preferred_element_type=jnp.float32
    )
    row_dot = jnp.sum(attn_probs * probs_grad, axis=-1, keepdims=True)
    scores_grad = (attn_probs * (probs_grad - row_dot)).astype(jnp.bfloat16)
    query_grad = jnp.einsum(
        "shqk,skhe->sqhe", scores_grad, keys_full, preferred_element_type=jnp.float32
    ) * HD ** (-0.5)
    key_term = jnp.einsum(
        "shqk,sqhe->skhe", scores_grad, queries, preferred_element_type=jnp.float32
    ) * HD ** (-0.5)
    return (query_grad, key_term, value_term)


def body(hidden_in, out_grad, norm_params, biases, attn_in, attn_out, mlp_up, mlp_down):
    seq_count, local_len = (hidden_in.shape[0], hidden_in.shape[1])
    row_count = seq_count * local_len
    small_params = (
        lax.all_gather(norm_params, ("dp", "seq"), axis=0, tiled=True),
        lax.all_gather(biases, ("dp", "seq"), axis=0, tiled=True),
    )
    norm_vec = small_params[0].astype(jnp.float32).reshape(4, D)
    bias_vec = small_params[1].astype(jnp.float32)
    pieces = (attn_in, attn_out, mlp_up, mlp_down)
    group_count = lax.axis_size("seq")
    share_index = lax.axis_index("seq")
    w_in, w_out, w_up, w_down = (
        lax.all_gather(pieces[0], "dp", axis=0, tiled=True),
        lax.all_gather(pieces[1], "dp", axis=1, tiled=True),
        lax.all_gather(pieces[2], "dp", axis=0, tiled=True),
        lax.all_gather(pieces[3], "dp", axis=1, tiled=True),
    )
    head_count = H // group_count
    col_width = 3 * D // group_count
    ff_width = FF // group_count
    in_bias = lax.dynamic_slice_in_dim(bias_vec, share_index * col_width, col_width)
    up_bias_vec = lax.dynamic_slice_in_dim(bias_vec, 3 * D + share_index * ff_width, ff_width)
    out_bias = bias_vec[3 * D + FF :]
    inputs = hidden_in.reshape(row_count, D).astype(jnp.float32)
    average = jnp.mean(inputs, axis=-1, keepdims=True)
    centered = inputs - average
    inv_std = lax.rsqrt(jnp.mean(centered * centered, axis=-1, keepdims=True) + norm_eps)
    normed = centered * inv_std
    attn_rows = (normed * norm_vec[0] + norm_vec[1]).astype(jnp.bfloat16)
    mlp_rows = (normed * norm_vec[2] + norm_vec[3]).astype(jnp.bfloat16)
    full_rows = (
        lax.all_gather(attn_rows.reshape(seq_count, local_len, D), "seq", axis=1, tiled=True),
        lax.all_gather(mlp_rows.reshape(seq_count, local_len, D), "seq", axis=1, tiled=True),
    )
    tok_len = local_len * group_count
    in_rows = full_rows[0].reshape(seq_count * tok_len, D)
    up_rows = full_rows[1].reshape(seq_count * tok_len, D)
    query_pos = jnp.arange(tok_len, dtype=jnp.int32)
    work_rows = seq_count * tok_len
    triple = jnp.dot(in_rows, w_in, preferred_element_type=jnp.float32) + in_bias
    split = triple.reshape(seq_count, tok_len, head_count, 3, HD)
    cosine_table, sine_table = rotary_tables(query_pos.astype(jnp.float32))
    queries = rotate(split[:, :, :, 0], cosine_table, sine_table).astype(jnp.bfloat16)
    key_rows = rotate(split[:, :, :, 1], cosine_table, sine_table).astype(jnp.bfloat16)
    value_rows = split[:, :, :, 2].astype(jnp.bfloat16)
    all_keys, all_values = (key_rows, value_rows)
    causal = query_pos[:, None] >= jnp.arange(all_keys.shape[1], dtype=jnp.int32)[None, :]
    mixed_heads, log_total = attend_forward(queries, all_keys, all_values, causal)
    mixed_rows = mixed_heads.reshape(work_rows, head_count * HD).astype(jnp.bfloat16)
    hidden = jnp.dot(up_rows, w_up, preferred_element_type=jnp.float32) + up_bias_vec
    activated = gelu(hidden).astype(jnp.bfloat16)
    partial_value = jnp.dot(mixed_rows, w_out, preferred_element_type=jnp.float32) + jnp.dot(
        activated, w_down, preferred_element_type=jnp.float32
    )
    branch_sum = lax.psum_scatter(
        partial_value.reshape(seq_count, tok_len, D), "seq", scatter_dimension=1, tiled=True
    ).reshape(row_count, D)
    layer_out = (inputs + branch_sum + out_bias).astype(jnp.bfloat16).reshape(hidden_in.shape)
    pieces_back = (attn_in, attn_out, mlp_up, mlp_down)
    w_in, w_out, w_up, w_down = (
        lax.all_gather(pieces_back[0], "dp", axis=0, tiled=True),
        lax.all_gather(pieces_back[1], "dp", axis=1, tiled=True),
        lax.all_gather(pieces_back[2], "dp", axis=0, tiled=True),
        lax.all_gather(pieces_back[3], "dp", axis=1, tiled=True),
    )
    cotangent = out_grad.reshape(row_count, D)
    cot_wide = cotangent.astype(jnp.float32)
    cot_rows = lax.all_gather(out_grad, "seq", axis=1, tiled=True).reshape(work_rows, D)
    down_term = jnp.dot(activated.T, cot_rows, preferred_element_type=jnp.float32)
    act_grad = jnp.dot(cot_rows, w_down.T, preferred_element_type=jnp.float32)
    hidden_grad = (act_grad * gelu_slope(hidden)).astype(jnp.bfloat16)
    up_term = jnp.dot(up_rows.T, hidden_grad, preferred_element_type=jnp.float32)
    up_sum = jnp.sum(hidden_grad.astype(jnp.float32), axis=0)
    mlp_rows_grad = jnp.dot(hidden_grad, w_up.T, preferred_element_type=jnp.float32)
    mixed_grad = jnp.dot(cot_rows, w_out.T, preferred_element_type=jnp.float32).astype(jnp.bfloat16)
    out_term = jnp.dot(mixed_rows.T, cot_rows, preferred_element_type=jnp.float32)
    query_grad, key_term, value_term = attend_backward(
        queries,
        all_keys,
        all_values,
        causal,
        log_total,
        mixed_grad.reshape(seq_count, tok_len, head_count, HD),
    )
    key_grad, value_grad = (key_term, value_term)
    triple_grad = (
        jnp.stack(
            [
                rotate_back(query_grad, cosine_table, sine_table),
                rotate_back(key_grad, cosine_table, sine_table),
                value_grad,
            ],
            axis=3,
        )
        .reshape(work_rows, col_width)
        .astype(jnp.bfloat16)
    )
    in_term = jnp.dot(in_rows.T, triple_grad, preferred_element_type=jnp.float32)
    triple_sum = jnp.sum(triple_grad.astype(jnp.float32), axis=0)
    attn_rows_grad = jnp.dot(triple_grad, w_in.T, preferred_element_type=jnp.float32)
    attn_grad_rows, mlp_grad_rows = (
        lax.psum_scatter(
            attn_rows_grad.reshape(seq_count, tok_len, D), "seq", scatter_dimension=1, tiled=True
        ),
        lax.psum_scatter(
            mlp_rows_grad.reshape(seq_count, tok_len, D), "seq", scatter_dimension=1, tiled=True
        ),
    )
    attn_grad_rows = attn_grad_rows.reshape(row_count, D)
    mlp_grad_rows = mlp_grad_rows.reshape(row_count, D)
    gain_attn = jnp.sum(attn_grad_rows * normed, axis=0)
    shift_attn = jnp.sum(attn_grad_rows, axis=0)
    gain_mlp = jnp.sum(mlp_grad_rows * normed, axis=0)
    shift_mlp = jnp.sum(mlp_grad_rows, axis=0)
    normed_grad = attn_grad_rows * norm_vec[0] + mlp_grad_rows * norm_vec[2]
    input_term = inv_std * (
        normed_grad
        - jnp.mean(normed_grad, axis=-1, keepdims=True)
        - normed * jnp.mean(normed_grad * normed, axis=-1, keepdims=True)
    )
    grad_input = (cot_wide + input_term).astype(jnp.bfloat16).reshape(hidden_in.shape)
    norm_term = jnp.stack([gain_attn, shift_attn, gain_mlp, shift_mlp]).reshape(-1)
    bias_term = jnp.zeros((4 * D + FF,), jnp.float32)
    bias_term = lax.dynamic_update_slice(bias_term, triple_sum, (share_index * col_width,))
    bias_term = lax.dynamic_update_slice(bias_term, up_sum, (3 * D + share_index * ff_width,))
    bias_term = lax.dynamic_update_slice(
        bias_term, jnp.sum(cot_wide, axis=0), (jnp.int32(3 * D + FF),)
    )
    norm_share, bias_share = (
        lax.psum_scatter(norm_term, ("dp", "seq"), scatter_dimension=0, tiled=True),
        lax.psum_scatter(bias_term, ("dp", "seq"), scatter_dimension=0, tiled=True),
    )
    reduced = (
        lax.psum_scatter(in_term, "dp", scatter_dimension=0, tiled=True),
        lax.psum_scatter(out_term, "dp", scatter_dimension=1, tiled=True),
        lax.psum_scatter(up_term, "dp", scatter_dimension=0, tiled=True),
        lax.psum_scatter(down_term, "dp", scatter_dimension=1, tiled=True),
    )
    in_share, out_share, up_share, down_share = reduced
    return (
        layer_out,
        grad_input,
        norm_share,
        bias_share,
        in_share,
        out_share,
        up_share,
        down_share,
    )


def solution(mesh):
    in_specs = (
        P("dp", "seq", None),
        P("dp", "seq", None),
        P(("dp", "seq")),
        P(("dp", "seq")),
        P("dp", "seq"),
        P("seq", "dp"),
        P("dp", "seq"),
        P("seq", "dp"),
    )
    out_specs = (
        P("dp", "seq", None),
        P("dp", "seq", None),
        P(("dp", "seq")),
        P(("dp", "seq")),
        P("dp", "seq"),
        P("seq", "dp"),
        P("dp", "seq"),
        P("seq", "dp"),
    )
    return jax.shard_map(body, mesh=mesh, in_specs=in_specs, out_specs=out_specs, check_vma=False)
```

profile of v0, /device:TPU:0, one launch (start us, length us, event | category | flops | bytes accessed | tf_op | source)
XLA Modules:
  0.0 567.5 jit_solution(8187904816132288084)
XLA Ops:
  8.0 69.7 %all-gather = bf16[32,1,128]{2,1,0:T(2,128)(2,1)S(1)} all-gather(bf16[1,1,128]{2,1,0:T(2,128)(2,1)} %bitcast.178), channel_id=1, replica_groups=mesh['dp'=8,'seq'=4] {'dp','seq'}, dimensions={0}, use_global_device_ids=true | all-gather | bytes 8448 | tf_op jit(solution)/shard_map/all_gather | solution.py:111
  79.9 2.0 fusion.29
  84.6 63.8 %all-gather.1 = bf16[32,1,256]{2,1,0:T(2,128)(2,1)S(1)} all-gather(bf16[1,1,256]{2,1,0:T(2,128)(2,1)S(1)} %reshape.461), channel_id=1, replica_groups=mesh['dp'=8,'seq'=4] {'dp','seq'}, dimensions={0}, use_global_device_ids=true | all-gather | bytes 16896 | tf_op jit(solution)/shard_map/all_gather | solution.py:112
  148.5 8.6 %all_gather.35 = bf16[256,1024]{1,0:T(8,128)(2,1)S(1)} all-gather(bf16[256,128]{1,0:T(8,128)(2,1)S(1)} %copy-done.14), channel_id=1, replica_groups=mesh['dp'=8,'seq'=4] {'dp'}, dimensions={1}, use_global_device_ids=true | all-gather | bytes 589824 | tf_op jit(solution)/shard_map/all_gather | solution.py:121
  157.4 1.7 convolution_convert_fusion
  159.1 3.9 convolution_add_fusion
  163.0 1.9 copy.32
  167.0 1.5 multiply_reduce_fusion
  168.5 1.3 multiply_convert_fusion
  171.2 1.2 convolution_bitcast_fusion.2
  174.1 2.4 convolution_bitcast_fusion.1
  176.9 15.8 %all-gather.15.cloned.1.call-done = bf16[1024,1024]{1,0:T(8,128)(2,1)} async-done(((bf16[128,1024]{1,0:T(8,128)(2,1)}), bf16[1024,1024]{1,0:T(8,128)(2,1)}) %all-gather.15.cloned.1.call-update) | async-done | bytes 2097168 | tf_op jit(solution)/shard_map/all_gather | solution.py:122
  192.7 4.9 multiply_convert_fusion.1
  197.6 25.0 %all-gather.17.cloned.1.call-done = bf16[1024,1024]{1,0:T(8,128)(2,1)} async-done(((bf16[1024,128]{1,0:T(8,128)(2,1)}), bf16[1024,1024]{1,0:T(8,128)(2,1)}) %all-gather.17.cloned.1.call-update) | async-done | bytes 2097168 | tf_op jit(solution)/shard_map/all_gather | solution.py:123
  222.6 4.2 convert_reduce_fusion
  227.8 2.6 convolution_bitcast_fusion
  230.5 3.6 convolution_convert_fusion.1
  234.1 1.3 fusion.67
  235.4 1.7 add_bitcast_fusion
  238.1 1.4 fusion.12
  239.6 2.8 fusion.20
  244.0 3.2 fusion.16
  248.4 3.3 fusion.10
  252.4 16.4 %reduce-scatter.10.cloned.1.call-done = f32[1,128,1024]{2,1,0:T(8,128)} async-done(((f32[1,512,1024]{2,1,0:T(8,128)}), f32[1,128,1024]{2,1,0:T(8,128)}) %reduce-scatter.10.cloned.1.call-update) | async-done | bytes 524304 | tf_op jit(solution)/shard_map/reduce_scatter | solution.py:209
  268.8 45.6 %reduce-scatter.12.cloned.1.call-done = f32[1,128,1024]{2,1,0:T(8,128)} async-done(((f32[1,512,1024]{2,1,0:T(8,128)}), f32[1,128,1024]{2,1,0:T(8,128)}) %reduce-scatter.12.cloned.1.call-update) | async-done | bytes 524304 | tf_op jit(solution)/shard_map/reduce_scatter | solution.py:212
  314.4 1.5 fusion.50
  316.0 44.0 %reduce-scatter.8.cloned.1.call-done = f32[1,128,1024]{2,1,0:T(8,128)} async-done(((f32[1,512,1024]{2,1,0:T(8,128)}), f32[1,128,1024]{2,1,0:T(8,128)}) %reduce-scatter.8.cloned.1.call-update) | async-done | bytes 524304 | tf_op jit(solution)/shard_map/reduce_scatter | solution.py:162
  360.0 2.5 fusion.65
  362.5 40.0 %all-reduce.2 = (f32[4096]{0:T(1024)S(1)}, f32[8192]{0:T(1024)S(1)}) all-reduce(f32[4096]{0:T(1024)S(1)} %bitcast.168, f32[8192]{0:T(1024)S(1)} %constant_dynamic-update-slice_fusion), channel_id=5, replica_groups=mesh['dp'=8,'seq'=4] {'dp','seq'}, use_global_device_ids=true, to_apply=%region_14.15.clone | all-reduce | flops 12288 | bytes 98304
  403.7 46.4 %reduce-scatter.14.cloned.1.call-done = f32[128,768]{1,0:T(8,128)} async-done(((f32[1024,768]{1,0:T(8,128)}), f32[128,768]{1,0:T(8,128)}) %reduce-scatter.14.cloned.1.call-update) | async-done | bytes 393232 | tf_op jit(solution)/shard_map/reduce_scatter | solution.py:241
  450.2 55.1 %reduce-scatter.18.cloned.1.call-done = f32[128,1024]{1,0:T(8,128)} async-done(((f32[1024,1024]{1,0:T(8,128)}), f32[128,1024]{1,0:T(8,128)}) %reduce-scatter.18.cloned.1.call-update) | async-done | bytes 524304 | tf_op jit(solution)/shard_map/reduce_scatter | solution.py:243
  505.3 55.6 %reduce-scatter.20.cloned.1.call-done = f32[1024,128]{1,0:T(8,128)} async-done(((f32[1024,1024]{1,0:T(8,128)}), f32[1024,128]{1,0:T(8,128)}) %reduce-scatter.20.cloned.1.call-update) | async-done | bytes 524304 | tf_op jit(solution)/shard_map/reduce_scatter | solution.py:244
  (112 shorter events, 18.0 us)
Async XLA Ops:
  7.2 77.5 %copy-start.18 = (bf16[256]{0:T(256)(128)(2,1)S(1)}, bf16[256]{0:T(256)(128)(2,1)}, u32[]{:S(2)}) copy-start(bf16[256]{0:T(256)(128)(2,1)} %param.11) | copy-start | bytes 1540
  7.2 141.3 %copy-start.14 = (bf16[256,128]{1,0:T(8,128)(2,1)S(1)}, bf16[256,128]{1,0:T(8,128)(2,1)}, u32[]{:S(2)}) copy-start(bf16[256,128]{1,0:T(8,128)(2,1)} %param.13) | copy-start | bytes 196612
  7.2 150.2 %all-gather.19.cloned.1.call-start = ((), (), s32[]{:S(2)}) async-start(), calls=%async_computation.13 | async-start | bytes 1310720 | tf_op jit(solution)/shard_map/all_gather | solution.py:175
  7.9 151.2 %all-gather.9.cloned.1.call-start = ((), (), s32[]{:S(2)}) async-start(), calls=%async_computation.7 | async-start | bytes 1310720 | tf_op jit(solution)/shard_map/all_gather | solution.py:139
  82.0 77.2 %all-gather.11.cloned.1.call-start = ((), (), s32[]{:S(2)}) async-start(), calls=%async_computation.8 | async-start | bytes 1769472 | tf_op jit(solution)/shard_map/all_gather | solution.py:120
  82.7 94.2 %all-gather.13.cloned.1.call-start = ((), (), s32[]{:S(2)}) async-start(), calls=%async_computation.9 | async-start | bytes 1310720 | tf_op jit(solution)/shard_map/all_gather | solution.py:140
  83.3 109.4 %all-gather.15.cloned.1.call-start = ((), (), s32[]{:S(2)}) async-start(), calls=%async_computation.10 | async-start | bytes 2359296 | tf_op jit(solution)/shard_map/all_gather | solution.py:122
  83.9 138.8 %all-gather.17.cloned.1.call-start = ((), (), s32[]{:S(2)}) async-start(), calls=%async_computation.11 | async-start | bytes 2359296 | tf_op jit(solution)/shard_map/all_gather | solution.py:123
  84.4 184.4 %reduce-scatter.10.cloned.1.call-start = ((), (), s32[]{:S(2)}) async-start(), calls=%async_computation.14 | async-start | bytes 2621440 | tf_op jit(solution)/shard_map/reduce_scatter | solution.py:209
  166.1 5.0 copy-start
  172.4 1.7 copy-start.17
  172.7 0.9 copy-start.4
  176.6 137.8 %reduce-scatter.12.cloned.1.call-start = ((), (), s32[]{:S(2)}) async-start(), calls=%async_computation.15 | async-start | bytes 2621440 | tf_op jit(solution)/shard_map/reduce_scatter | solution.py:212
  176.8 45.8 %copy-start.2 = (bf16[1,512,1024]{2,1,0:T(8,128)(2,1)S(1)}, bf16[1,512,1024]{2,1,0:T(8,128)(2,1)}, u32[]{:S(2)}) copy-start(bf16[1,512,1024]{2,1,0:T(8,128)(2,1)} %all-gather.19.cloned.1.call-done) | copy-start | bytes 3145732
  222.6 5.1 copy-start.16
  226.8 1.0 copy-start.12
  230.4 129.6 %reduce-scatter.8.cloned.1.call-start = ((), (), s32[]{:S(2)}) async-start(), calls=%async_computation.12 | async-start | bytes 2621440 | tf_op jit(solution)/shard_map/reduce_scatter | solution.py:162
  230.4 3.7 copy-start.7
  230.4 3.7 copy-start.15
  234.1 1.3 copy-start.9
  237.1 1.0 copy-start.10
  237.2 2.4 copy-start.3
  237.2 2.4 copy-start.5
  237.2 166.5 %reduce-scatter.16.cloned.1.call-start = ((), (), s32[]{:S(2)}) async-start(), calls=%async_computation.17 | async-start | bytes 1179648 | tf_op jit(solution)/shard_map/reduce_scatter | solution.py:242
  239.6 210.6 %reduce-scatter.14.cloned.1.call-start = ((), (), s32[]{:S(2)}) async-start(), calls=%async_computation.16 | async-start | bytes 3538944 | tf_op jit(solution)/shard_map/reduce_scatter | solution.py:241
  242.4 1.2 copy-start.6
  242.4 1.6 copy-start.13
  242.4 262.9 %reduce-scatter.18.cloned.1.call-start = ((), (), s32[]{:S(2)}) async-start(), calls=%async_computation.18 | async-start | bytes 4718592 | tf_op jit(solution)/shard_map/reduce_scatter | solution.py:243
  247.2 1.2 copy-start.8
  247.2 313.7 %reduce-scatter.20.cloned.1.call-start = ((), (), s32[]{:S(2)}) async-start(), calls=%async_computation.19 | async-start | bytes 4718592 | tf_op jit(solution)/shard_map/reduce_scatter | solution.py:244
  251.7 62.7 %copy-start.1 = (bf16[1,128,1024]{2,1,0:T(8,128)(2,1)S(1)}, bf16[1,128,1024]{2,1,0:T(8,128)(2,1)}, u32[]{:S(2)}) copy-start(bf16[1,128,1024]{2,1,0:T(8,128)(2,1)} %param.8) | copy-start | bytes 786436
  251.7 108.3 %copy-start.11 = (bf16[1,128,1024]{2,1,0:T(8,128)(2,1)S(1)}, bf16[1,128,1024]{2,1,0:T(8,128)(2,1)}, u32[]{:S(2)}) copy-start(bf16[1,128,1024]{2,1,0:T(8,128)(2,1)} %param.9) | copy-start | bytes 786436
Sparse Core Ops, SparseCore 0:
  9.6 30.7 all-gather.18
  82.1 24.2 all-gather.8
  108.2 25.1 all-gather.10
  135.5 27.9 all-gather.12
  165.2 27.4 all-gather.14
  194.4 28.1 all-gather.16
  224.9 43.8 reduce-scatter.9
  271.2 43.1 reduce-scatter.11
  316.7 43.1 reduce-scatter.7
  363.9 35.4 reduce-scatter.15
  403.7 46.3 reduce-scatter.13
  453.9 51.3 reduce-scatter.17
  509.6 51.2 reduce-scatter.19
where the time goes:
time: 568 us; the launch traced here: 567 us
  waiting for transfers between devices  307 us (54%)
  blocking collectives  182 us (32%)
  matrix products  41.9 us (7%)
  between operations  14.4 us (3%)
  other arithmetic  11.1 us (2%)
  local copies, waits for them, and re-layouts  10.1 us (2%)
    all_gather x1, blocking collectives, body(): lax.all_gather(norm_params, ('dp', 'seq'), axis=0, tiled=True)  69.7 us
    all_gather x1, blocking collectives, body(): lax.all_gather(biases, ('dp', 'seq'), axis=0, tiled=True)  63.8 us
    reduce_scatter x1, waiting for transfers between devices, body(): lax.psum_scatter(down_term, 'dp', scatter_dimension=1, tiled=True)  55.6 us
    reduce_scatter x1, waiting for transfers between devices, body(): lax.psum_scatter(up_term, 'dp', scatter_dimension=0, tiled=True)  55.1 us
    reduce_scatter x1, waiting for transfers between devices, body(): lax.psum_scatter(in_term, 'dp', scatter_dimension=0, tiled=True)  46.4 us
    reduce_scatter x1, waiting for transfers between devices, body(): lax.psum_scatter(mlp_rows_grad.reshape(seq_count, tok_len, D), 'seq', sca...  45.6 us
    reduce_scatter x1, waiting for transfers between devices, body(): lax.psum_scatter(partial_value.reshape(seq_count, tok_len, D), 'seq', sca...  44 us
    unnamed x1, blocking collectives  40 us
  transfers between devices with their start and end apart: 13, of which 8 were waited for; matrix products, arithmetic and copies ran while one was open for 10% of the time, Pallas kernels for 0%

commit v1 on v0

v1 whole, which is shorter than its diff:
```python
import functools
import math

import jax
import jax.numpy as jnp
from jax import lax
from jax.experimental import pallas as pl
from jax.experimental.pallas import tpu as pltpu
from jax.sharding import PartitionSpec as P

D = 1024
H = 16
HD = 64
FF = 4096
ROT = 16


norm_eps = 1e-05
masked_score = -1e30


def rotary_tables(positions):
    half_rot = ROT // 2
    frequency = jnp.power(
        jnp.float32(10000.0), -2.0 * jnp.arange(half_rot, dtype=jnp.float32) / ROT
    )
    angles = positions[:, None] * frequency[None, :]
    return (jnp.cos(angles)[:, None, :], jnp.sin(angles)[:, None, :])


def rotate(tensor, cosine_table, sine_table):
    half_rot = ROT // 2
    first_half = tensor[..., :half_rot]
    second = tensor[..., half_rot:ROT]
    untouched = tensor[..., ROT:]
    return jnp.concatenate(
        [
            first_half * cosine_table - second * sine_table,
            second * cosine_table + first_half * sine_table,
            untouched,
        ],
        axis=-1,
    )


def rotate_back(tensor, cosine_table, sine_table):
    half_rot = ROT // 2
    first_half = tensor[..., :half_rot]
    second = tensor[..., half_rot:ROT]
    untouched = tensor[..., ROT:]
    return jnp.concatenate(
        [
            first_half * cosine_table + second * sine_table,
            second * cosine_table - first_half * sine_table,
            untouched,
        ],
        axis=-1,
    )


def gelu(values):
    return 0.5 * values * (1.0 + jax.scipy.special.erf(values * (1.0 / math.sqrt(2.0))))


def gelu_slope(values):
    return 0.5 * (1.0 + jax.scipy.special.erf(values * (1.0 / math.sqrt(2.0)))) + values * jnp.exp(
        -0.5 * values * values
    ) * (1.0 / math.sqrt(2.0 * math.pi))


def score_block(queries, keys_full, causal):
    raw_scores = jnp.einsum(
        "sqhe,skhe->shqk", queries, keys_full, preferred_element_type=jnp.float32
    ) * HD ** (-0.5)
    return jnp.where(causal, raw_scores, masked_score)


def attend_forward(queries, keys_full, values_full, causal):
    scores = score_block(queries, keys_full, causal)
    row_max = jnp.max(scores, axis=-1, keepdims=True)
    log_total = row_max + jnp.log(jnp.sum(jnp.exp(scores - row_max), axis=-1, keepdims=True))
    probs_low = jnp.exp(scores - log_total).astype(jnp.bfloat16)
    mixed_heads = jnp.einsum(
        "shqk,skhe->sqhe", probs_low, values_full, preferred_element_type=jnp.float32
    )
    return (mixed_heads, log_total)


def attend_backward(queries, keys_full, values_full, causal, log_total, mixed_heads):
    scores = score_block(queries, keys_full, causal)
    attn_probs = jnp.exp(scores - log_total)
    probs_low = attn_probs.astype(jnp.bfloat16)
    probs_grad = jnp.einsum(
        "sqhe,skhe->shqk", mixed_heads, values_full, preferred_element_type=jnp.float32
    )
    value_term = jnp.einsum(
        "shqk,sqhe->skhe", probs_low, mixed_heads, preferred_element_type=jnp.float32
    )
    row_dot = jnp.sum(attn_probs * probs_grad, axis=-1, keepdims=True)
    scores_grad = (attn_probs * (probs_grad - row_dot)).astype(jnp.bfloat16)
    query_grad = jnp.einsum(
        "shqk,skhe->sqhe", scores_grad, keys_full, preferred_element_type=jnp.float32
    ) * HD ** (-0.5)
    key_term = jnp.einsum(
        "shqk,sqhe->skhe", scores_grad, queries, preferred_element_type=jnp.float32
    ) * HD ** (-0.5)
    return (query_grad, key_term, value_term)


MESH = pl.DeviceIdType.MESH


def places(chips, groups):
    dp, z = lax.axis_index("dp"), lax.axis_index("seq")
    chip, core = dp // 2, dp % 2
    partner = {"dp": chip * 2 + (1 - core)}
    across = [{"dp": (chip + k) % chips * 2 + core} for k in range(chips)]
    along = [{"seq": (z + k) % groups} for k in range(groups)]
    return chip, core, z, partner, across, along


def greet(partner, across, along):
    barrier = pltpu.get_barrier_semaphore()
    peers = [partner] + across[1:] + along[1:]
    for peer in peers:
        pl.semaphore_signal(barrier, inc=1, device_id=peer, device_id_type=MESH)
    pl.semaphore_wait(barrier, len(peers))


def gather_kernel(
    chips, groups, w_ref, x_ref, c_ref, s_ref, w_all, x_all, c_all, s_all,
    local_sem, w_send, w_recv, p_send, p_recv, z_send, z_recv, sa_send, sa_recv, sp_send, sp_recv,
):
    chip, core, z, partner, across, along = places(chips, groups)
    mine = chip * 2 + core
    local = [
        pltpu.make_async_copy(w_ref, w_all.at[mine], local_sem.at[0]),
        pltpu.make_async_copy(x_ref, x_all.at[z], local_sem.at[1]),
        pltpu.make_async_copy(c_ref, c_all.at[z], local_sem.at[2]),
        pltpu.make_async_copy(s_ref, s_all.at[mine, z], local_sem.at[3]),
    ]
    for copy in local:
        copy.start()
    greet(partner, across, along)

    def remote(source, target, send, recv, peer):
        return pltpu.make_async_remote_copy(
            src_ref=source, dst_ref=target, send_sem=send, recv_sem=recv,
            device_id=peer, device_id_type=MESH,
        )

    smalls, rows, cots, blocks, handed, small_out = [], [], [], [], [], []
    for k in range(1, groups):
        smalls.append(remote(s_ref, s_all.at[mine, z], z_send.at[0, k], z_recv.at[0, k], along[k]))
        smalls[-1].start()
    for k in range(1, chips):
        blocks.append(remote(w_ref, w_all.at[mine], w_send.at[k], w_recv.at[k], across[k]))
        blocks[-1].start()
    handed.append(remote(w_ref, w_all.at[mine], p_send.at[0], p_recv.at[0], partner))
    handed[-1].start()
    for k in range(1, groups):
        rows.append(remote(x_ref, x_all.at[z], z_send.at[1, k], z_recv.at[1, k], along[k]))
        rows[-1].start()
    for k in range(1, groups):
        cots.append(remote(c_ref, c_all.at[z], z_send.at[2, k], z_recv.at[2, k], along[k]))
        cots[-1].start()
    for copy in smalls:
        copy.wait_recv()
    local[3].wait()
    for k in range(1, chips):
        small_out.append(remote(s_all.at[mine], s_all.at[mine], sa_send.at[k], sa_recv.at[k], across[k]))
        small_out[-1].start()
    small_pass = [remote(s_all.at[mine], s_all.at[mine], sp_send.at[0], sp_recv.at[0], partner)]
    small_pass[0].start()
    for k in range(1, chips):
        small_out[k - 1].wait_recv()
        came = (chip + chips - k) % chips * 2 + core
        small_pass.append(remote(s_all.at[came], s_all.at[came], sp_send.at[k], sp_recv.at[k], partner))
        small_pass[-1].start()
    for k in range(1, chips):
        blocks[k - 1].wait_recv()
        came = (chip + chips - k) % chips * 2 + core
        handed.append(remote(w_all.at[came], w_all.at[came], p_send.at[k], p_recv.at[k], partner))
        handed[-1].start()
    for copy in handed + small_pass + rows + cots:
        copy.wait_recv()
    for copy in smalls + small_out + small_pass + blocks + handed + rows + cots:
        copy.wait_send()
    for copy in local[:3]:
        copy.wait()


def gather_all(w, x, c, s, chips, groups):
    any_spec = pl.BlockSpec(memory_space=pl.ANY)
    dma = pltpu.SemaphoreType.DMA
    return pl.pallas_call(
        functools.partial(gather_kernel, chips, groups),
        out_shape=(
            jax.ShapeDtypeStruct((2 * chips,) + w.shape, w.dtype),
            jax.ShapeDtypeStruct((groups,) + x.shape, x.dtype),
            jax.ShapeDtypeStruct((groups,) + c.shape, c.dtype),
            jax.ShapeDtypeStruct((2 * chips, groups) + s.shape, s.dtype),
        ),
        in_specs=[any_spec] * 4,
        out_specs=(any_spec,) * 4,
        scratch_shapes=[
            dma((4,)), dma((chips,)), dma((chips,)), dma((chips,)), dma((chips,)),
            dma((3, groups)), dma((3, groups)),
            dma((chips,)), dma((chips,)), dma((chips,)), dma((chips,)),
        ],
        compiler_params=pltpu.CompilerParams(collective_id=0, has_side_effects=True),
        name="gather_all",
    )(w, x, c, s)


def reduce_kernel(
    chips, groups, g_ref, p_ref, n_ref, v_ref, g_out, p_out, n_out, v_out,
    g_half, g_sum, g_got, p_got, n_got, v_half, v_sum, v_got, v_all, vz_got,
    h_send, h_recv, a_send, a_recv, z_send, z_recv, vh_send, vh_recv, va_send, va_recv, vz_send, vz_recv,
):
    chip, core, z, partner, across, along = places(chips, groups)
    greet(partner, across, along)

    def remote(source, target, send, recv, peer):
        return pltpu.make_async_remote_copy(
            src_ref=source, dst_ref=target, send_sem=send, recv_sem=recv,
            device_id=peer, device_id_type=MESH,
        )

    f32 = jnp.float32
    order = list(range(1, chips)) + [0]
    v_give = remote(v_ref.at[1 - core], v_half, vh_send.at[0], vh_recv.at[0], partner)
    v_give.start()
    halves = {}
    for k in order:
        at = (chip + k) % chips
        halves[k] = remote(g_ref.at[at * 2 + 1 - core], g_half.at[k], h_send.at[k], h_recv.at[k], partner)
        halves[k].start()
    rows = []
    for k in range(1, groups):
        to = (z + k) % groups
        rows.append(remote(p_ref.at[to], p_got.at[k], z_send.at[0, k], z_recv.at[0, k], along[k]))
        rows[-1].start()
        rows.append(remote(n_ref.at[to], n_got.at[k], z_send.at[1, k], z_recv.at[1, k], along[k]))
        rows[-1].start()
    v_give.wait_recv()
    v_sum[...] = v_ref[core] + v_half[...]
    v_across = []
    for k in range(1, chips):
        at = (chip + k) % chips
        v_across.append(remote(v_sum.at[at], v_got.at[k], va_send.at[k], va_recv.at[k], across[k]))
        v_across[-1].start()
    sums = []
    for k in order:
        at = (chip + k) % chips
        halves[k].wait_recv()
        both = g_ref[at * 2 + core].astype(f32) + g_half[k].astype(f32)
        if k > 0:
            g_sum[k] = both.astype(g_sum.dtype)
            sums.append(remote(g_sum.at[k], g_got.at[k], a_send.at[k], a_recv.at[k], across[k]))
            sums[-1].start()
        else:
            g_out[...] = both
    for copy in v_across:
        copy.wait_recv()
    total = v_sum[chip]
    for k in range(1, chips):
        total = total + v_got[k]
    v_all[...] = total
    v_along = []
    for k in range(1, groups):
        to = (z + k) % groups
        v_along.append(remote(v_all.at[to], vz_got.at[k], vz_send.at[k], vz_recv.at[k], along[k]))
        v_along[-1].start()
    for copy in rows:
        copy.wait_recv()
    p_out[...] = p_ref[z].astype(f32)
    n_out[...] = n_ref[z].astype(f32)
    for k in range(1, groups):
        p_out[...] += p_got[k].astype(f32)
        n_out[...] += n_got[k].astype(f32)
    for copy in v_along:
        copy.wait_recv()
    total = v_all[z]
    for k in range(1, groups):
        total = total + vz_got[k]
    v_out[...] = total
    for k in range(1, chips):
        sums[k - 1].wait_recv()
        g_out[...] += g_got[k].astype(f32)
    for copy in [v_give] + list(halves.values()) + rows + v_across + sums + v_along:
        copy.wait_send()


def reduce_all(g, p, n, v, chips, groups):
    vm = pl.BlockSpec(memory_space=pltpu.VMEM)
    dma = pltpu.SemaphoreType.DMA
    block, rows, small = g.shape[1:], p.shape[1:], v.shape[3:]
    f32 = jnp.float32
    return pl.pallas_call(
        functools.partial(reduce_kernel, chips, groups),
        out_shape=(
            jax.ShapeDtypeStruct(block, f32),
            jax.ShapeDtypeStruct(rows, f32),
            jax.ShapeDtypeStruct(rows, f32),
            jax.ShapeDtypeStruct(small, f32),
        ),
        in_specs=[vm] * 4,
        out_specs=(vm,) * 4,
        scratch_shapes=[
            pltpu.VMEM((chips,) + block, g.dtype),
            pltpu.VMEM((chips,) + block, g.dtype),
            pltpu.VMEM((chips,) + block, g.dtype),
            pltpu.VMEM((groups,) + rows, p.dtype),
            pltpu.VMEM((groups,) + rows, p.dtype),
            pltpu.VMEM((chips, groups) + small, f32),
            pltpu.VMEM((chips, groups) + small, f32),
            pltpu.VMEM((chips, groups) + small, f32),
            pltpu.VMEM((groups,) + small, f32),
            pltpu.VMEM((groups,) + small, f32),
            dma((chips,)), dma((chips,)), dma((chips,)), dma((chips,)),
            dma((2, groups)), dma((2, groups)),
            dma((1,)), dma((1,)), dma((chips,)), dma((chips,)), dma((groups,)), dma((groups,)),
        ],
        compiler_params=pltpu.CompilerParams(
            collective_id=1, has_side_effects=True, vmem_limit_bytes=48 * 2**20
        ),
        name="reduce_all",
    )(g, p, n, v)


def body(hidden_in, out_grad, norm_params, biases, attn_in, attn_out, mlp_up, mlp_down):
    local_len = hidden_in.shape[1]
    groups, devices = lax.axis_size("seq"), lax.axis_size("dp")
    chips = devices // 2
    z = lax.axis_index("seq")
    f32, bf16 = jnp.float32, jnp.bfloat16
    heads, col_width, ff_width = H // groups, 3 * D // groups, FF // groups
    out_width = D // groups
    norm_size, bias_size = norm_params.shape[0], biases.shape[0]
    small_size = norm_size + bias_size
    small_pad = -small_size % 128

    packed = jnp.concatenate([attn_in, attn_out.T, mlp_up, mlp_down.T], axis=1)
    small = jnp.pad(jnp.concatenate([norm_params, biases]), (0, small_pad))
    small = jnp.broadcast_to(small[None, :], (16, small_size + small_pad))
    w_all, x_all, c_all, s_all = gather_all(packed, hidden_in[0], out_grad[0], small, chips, groups)
    tok_len = local_len * groups
    w = w_all.reshape(D, -1)
    w_in = w[:, :col_width]
    w_out_t = w[:, col_width : col_width + out_width]
    w_up = w[:, col_width + out_width : col_width + out_width + ff_width]
    w_down_t = w[:, col_width + out_width + ff_width :]
    small_rows = s_all[:, :, 0, :].astype(f32)
    norm_vec = small_rows[:, :, :norm_size].reshape(4, D)
    bias_vec = small_rows[:, :, norm_size:small_size].reshape(-1)
    in_bias = lax.dynamic_slice_in_dim(bias_vec, z * col_width, col_width)
    up_bias = lax.dynamic_slice_in_dim(bias_vec, 3 * D + z * ff_width, ff_width)
    out_bias = bias_vec[3 * D + FF :]

    cot = c_all.reshape(tok_len, D)
    inputs = x_all.reshape(tok_len, D).astype(f32)
    average = jnp.mean(inputs, axis=-1, keepdims=True)
    centered = inputs - average
    inv_std = lax.rsqrt(jnp.mean(centered * centered, axis=-1, keepdims=True) + norm_eps)
    normed = centered * inv_std
    attn_rows = (normed * norm_vec[0] + norm_vec[1]).astype(bf16)
    mlp_rows = (normed * norm_vec[2] + norm_vec[3]).astype(bf16)

    def mul(a, b, ca, cb):
        return lax.dot_general(a, b, (((ca,), (cb,)), ((), ())), preferred_element_type=f32)

    triple = mul(attn_rows, w_in, 1, 0) + in_bias
    split = triple.reshape(1, tok_len, heads, 3, HD)
    query_pos = jnp.arange(tok_len, dtype=jnp.int32)
    cosine_table, sine_table = rotary_tables(query_pos.astype(f32))
    queries = rotate(split[:, :, :, 0], cosine_table, sine_table).astype(bf16)
    key_rows = rotate(split[:, :, :, 1], cosine_table, sine_table).astype(bf16)
    value_rows = split[:, :, :, 2].astype(bf16)
    causal = query_pos[:, None] >= query_pos[None, :]
    mixed_heads, log_total = attend_forward(queries, key_rows, value_rows, causal)
    mixed_rows = mixed_heads.reshape(tok_len, heads * HD).astype(bf16)
    hidden = mul(mlp_rows, w_up, 1, 0) + up_bias
    activated = gelu(hidden).astype(bf16)
    branch = mul(mixed_rows, w_out_t, 1, 1) + mul(activated, w_down_t, 1, 1)

    down_term = mul(cot, activated, 0, 0)
    hidden_grad = (mul(cot, w_down_t, 1, 0) * gelu_slope(hidden)).astype(bf16)
    up_term = mul(mlp_rows, hidden_grad, 0, 0)
    up_sum = jnp.sum(hidden_grad.astype(f32), axis=0)
    mlp_grad = mul(hidden_grad, w_up, 1, 1)
    mixed_grad = mul(cot, w_out_t, 1, 0).astype(bf16)
    out_term = mul(cot, mixed_rows, 0, 0)
    query_grad, key_grad, value_grad = attend_backward(
        queries, key_rows, value_rows, causal, log_total, mixed_grad.reshape(1, tok_len, heads, HD)
    )
    triple_grad = (
        jnp.stack(
            [
                rotate_back(query_grad, cosine_table, sine_table),
                rotate_back(key_grad, cosine_table, sine_table),
                value_grad,
            ],
            axis=3,
        )
        .reshape(tok_len, col_width)
        .astype(bf16)
    )
    in_term = mul(attn_rows, triple_grad, 0, 0)
    triple_sum = jnp.sum(triple_grad.astype(f32), axis=0)
    attn_grad = mul(triple_grad, w_in, 1, 1)
    normed_grad = attn_grad * norm_vec[0] + mlp_grad * norm_vec[2]

    norm_term = jnp.stack(
        [
            jnp.sum(attn_grad * normed, axis=0),
            jnp.sum(attn_grad, axis=0),
            jnp.sum(mlp_grad * normed, axis=0),
            jnp.sum(mlp_grad, axis=0),
        ]
    ).reshape(devices, groups, norm_size)
    cot_own = out_grad[0].astype(f32)
    bias_term = jnp.zeros((4 * D + FF,), f32)
    bias_term = lax.dynamic_update_slice(bias_term, triple_sum, (z * col_width,))
    bias_term = lax.dynamic_update_slice(bias_term, up_sum, (3 * D + z * ff_width,))
    bias_term = lax.dynamic_update_slice(bias_term, jnp.sum(cot_own, axis=0), (jnp.int32(3 * D + FF),))
    small_pad = -small_size % 1024
    v = jnp.concatenate([norm_term, bias_term.reshape(devices, groups, bias_size)], axis=2)
    v = jnp.pad(v, ((0, 0), (0, 0), (0, small_pad)))
    v = v.reshape(chips, 2, groups, (small_size + small_pad) // 128, 128).transpose(1, 0, 2, 3, 4)

    g = jnp.concatenate([in_term, out_term, up_term, down_term], axis=1).astype(bf16)
    g = g.reshape(devices, D // devices, -1)
    g_sum, branch_sum, normed_grad, v_sum = reduce_all(
        g,
        branch.astype(bf16).reshape(groups, local_len, D),
        normed_grad.astype(bf16).reshape(groups, local_len, D),
        v,
        chips,
        groups,
    )
    own = hidden_in[0].astype(f32)
    layer_out = (own + branch_sum + out_bias).astype(bf16)[None]
    own_average = jnp.mean(own, axis=-1, keepdims=True)
    own_centered = own - own_average
    own_std = lax.rsqrt(jnp.mean(own_centered * own_centered, axis=-1, keepdims=True) + norm_eps)
    own_normed = own_centered * own_std
    input_term = own_std * (
        normed_grad
        - jnp.mean(normed_grad, axis=-1, keepdims=True)
        - own_normed * jnp.mean(normed_grad * own_normed, axis=-1, keepdims=True)
    )
    grad_input = (cot_own + input_term).astype(bf16)[None]
    flat = v_sum.reshape(-1)
    return (
        layer_out,
        grad_input,
        flat[:norm_size],
        flat[norm_size:small_size],
        g_sum[:, :col_width],
        g_sum[:, col_width : col_width + out_width].T,
        g_sum[:, col_width + out_width : col_width + out_width + ff_width],
        g_sum[:, col_width + out_width + ff_width :].T,
    )


def solution(mesh):
    in_specs = (
        P("dp", "seq", None),
        P("dp", "seq", None),
        P(("dp", "seq")),
        P(("dp", "seq")),
        P("dp", "seq"),
        P("seq", "dp"),
        P("dp", "seq"),
        P("seq", "dp"),
    )
    out_specs = (
        P("dp", "seq", None),
        P("dp", "seq", None),
        P(("dp", "seq")),
        P(("dp", "seq")),
        P("dp", "seq"),
        P("seq", "dp"),
        P("dp", "seq"),
        P("seq", "dp"),
    )
    return jax.shard_map(body, mesh=mesh, in_specs=in_specs, out_specs=out_specs, check_vma=False)
```

time: 568 us -> 186 us (0.33)
  waiting for transfers between devices: 307 us -> 0 us
  blocking collectives: 182 us -> 0 us
  Pallas kernels: 0 us -> 107 us
  between operations: 14.4 us -> 1.2 us
  local copies, waits for them, and re-layouts: 10.1 us -> 21.4 us
  other arithmetic: 11.1 us -> 17.3 us
    reduce_scatter x7 -> x0, waiting for transfers between devices: 263 us -> none  [the longest x1 55.6 us: body(): lax.psum_scatter(down_term, 'dp', scatter_dimension=1, tiled=True)]
    all_gather x3 -> x0, blocking collectives: 142 us -> none  [the longest x1 69.7 us: body(): lax.all_gather(norm_params, ('dp', 'seq'), axis=0, tiled=True)]
    pallas_call x0 -> x2, Pallas kernels: none -> 107 us  [the longest x1 54.3 us: reduce_all(): pl.pallas_call(functools.partial(reduce_kernel, chips, groups), out_shape...]
    all_gather x6 -> x0, waiting for transfers between devices: 40.9 us -> none  [the longest x1 25 us: body(): lax.all_gather(pieces[3], 'dp', axis=1, tiled=True)]
    unnamed x1 -> x0, blocking collectives: 40 us -> none
  transfers between devices with their start and end apart: 13 -> 0, of which waited for: 8 -> 0; matrix products, arithmetic and copies ran while one was open for 10% -> 0% of each run, Pallas kernels for 0% -> 0%
where the time goes in v1:
time: 186 us; the launch traced here: 185 us
  Pallas kernels  107 us (58%)
  matrix products  38.1 us (20%)
  local copies, waits for them, and re-layouts  21.4 us (12%)
  other arithmetic  17.3 us (9%)
    pallas_call x1, Pallas kernels, reduce_all(): pl.pallas_call(functools.partial(reduce_kernel, chips, groups), out_shape...  54.3 us
    pallas_call x1, Pallas kernels, gather_all(): pl.pallas_call(functools.partial(gather_kernel, chips, groups), out_shape...  52.9 us
    dot_general x12, matrix products, mul(): lax.dot_general(a, b, (((ca,), (cb,)), ((), ())), preferred_element_type=...  29.8 us
    unnamed x57, local copies, waits for them, and re-layouts  8.59 us
    dot_general x3, local copies, waits for them, and re-layouts, mul(): lax.dot_general(a, b, (((ca,), (cb,)), ((), ())), preferred_element_type=...  5.31 us

profile of v1, /device:TPU:0, one launch (start us, length us, event | category | flops | bytes accessed | tf_op | source)
XLA Modules:
  0.0 185.0 jit_solution(1402358760264426500)
XLA Ops:
  0.7 1.1 copy.71
  2.7 1.9 %pad_maximum_fusion.1.w_ref = bf16[128,3072]{1,0:T(8,128)(2,1)} fusion(bf16[128,1024]{1,0:T(8,128)(2,1)S(1)} %bitcast.165, bf16[128,1024]{1,0:T(8,128)(2,1)} %param.14, bf16[128,256]{1,0:T(8,128)(2,1)S(1)} %bitcast.172, bf16[128,768]{1,0:T(8,128)(2,1)} %param.12), kind=kLoop, calls=%fused_computation.57 | loop fusion | flops 3145728 | bytes 1572864 | tf_op jit(solution)/shard_map/concatenate | solution.py:344
  5.3 52.9 %gather_all.1 = (bf16[8,128,3072]{2,1,0:T(8,128)(2,1)}, bf16[4,128,1024]{2,1,0:T(8,128)(2,1)}, bf16[4,128,1024]{2,1,0:T(8,128)(2,1)}, bf16[8,4,16,384]{3,2,1,0:T(8,128)(2,1)}) custom-call(bf16[128,3072]{1,0:T(8,128)(2,1)} %pad_maximum_fusion.1.w_ref, bf16[128,1024]{1,0:T(8,128)(2,1)} %bitcast.151, bf16[128,1024]{1,0:T(8,128)(2,1)} %bitcast.159, ...), custom_call_target="tpu_custom_call" | custom-call | tf_op jit(solution)/shard_map/gather_all/pallas_call | solution.py:196
  58.2 1.5 convert_reduce_fusion.1
  59.7 1.6 multiply_reduce_fusion.3
  63.0 1.6 add_convert_fusion.3
  64.7 3.5 %convolution_add_fusion = f32[512,768]{1,0:T(8,128)} fusion(bf16[512,1024]{1,0:T(8,128)(2,1)S(1)} %get-tuple-element.71, bf16[1024,3072]{1,0:T(8,128)(2,1)} %bitcast.178, f32[768]{0:T(1024)S(1)} %dynamic_slice.6), kind=kOutput, calls=%fused_computation.42 | convolution fusion | flops 805699584 | bytes 4197376 | tf_op jit(solution)/shard_map/dot_general | solution.py:371
  68.2 1.9 %copy.73 = f32[512,768]{0,1:T(8,128)S(1)} copy(f32[512,768]{1,0:T(8,128)} %convolution_add_fusion) | data formatting | bytes 3145728 | tf_op jit(solution)/shard_map/add | solution.py:373
  72.6 1.0 copy-done.8
  73.6 1.5 convolution_convert_fusion.5
  75.1 1.5 multiply_reduce_fusion
  76.6 1.3 multiply_convert_fusion
  79.2 1.3 convolution_bitcast_fusion
  80.7 1.0 copy.80
  81.7 4.5 %multiply_convert_fusion.1 = (bf16[512,1024]{1,0:T(8,128)(2,1)}, f32[512,1024]{1,0:T(8,128)S(1)}) fusion(f32[1024]{0:T(1024)S(1)} %dynamic_slice.7, bf16[512,1024]{1,0:T(8,128)(2,1)} %get-tuple-element.72, bf16[1024,3072]{1,0:T(8,128)(2,1)} %bitcast.180), kind=kOutput, calls=%fused_computation.22 | convolution fusion | flops 1076887552 | bytes 6295552 | tf_op jit(solution)/shard_map/dot_general | solution.py:371
  86.2 3.8 %convert_reduce_fusion = (f32[1024]{0:T(1024)S(1)}, bf16[512,1024]{1,0:T(8,128)(2,1)S(1)}) fusion(f32[512,1024]{1,0:T(8,128)S(1)} %get-tuple-element.98, f32[1024]{0:T(1024)S(1)} %dynamic_slice.7, bf16[512,1024]{1,0:T(8,128)(2,1)S(1)} %bitcast.162, bf16[1024,3072]{1,0:T(8,128)(2,1)} %bitcast.181), kind=kOutput, calls=%fused_computation.17 | convolution fusion | flops 1080556544 | bytes 6299648 | tf_op jit(solution)/shard_map/dot_general | solution.py:371
  91.0 1.3 fusion.9
  92.3 2.7 %multiply_reduce_fusion.2 = (f32[1024]{0:T(1024)S(1)}, f32[1024]{0:T(1024)S(1)}, f32[1024]{0:T(1024)S(1)}, f32[1024]{0:T(1024)S(1)}, bf16[512,1024]{1,0:T(8,128)(2,1)}) fusion(bf16[4,128,1024]{2,1,0:T(8,128)(2,1)S(1)} %copy-done.4, f32[512]{0:T(512)S(1)} %get-tuple-element.94, f32[512]{0:T(512)S(1)} %get-tuple-element.95, f32[512,1024]{1,0:T(8,128)S(1)} %fusion.9, ...), kind=kOutput, calls=%fused_computation.19 | convolution fusion | flops 812118016 | bytes 6582272 | tf_op jit(solution)/shard_map/dot_general | solution.py:371
  95.9 3.4 %convolution_convert_fusion.4 = bf16[4,64,512]{2,1,0:T(8,128)(2,1)S(1)} fusion(f32[4,512,512]{1,2,0:T(8,128)} %copy-done.3, f32[4,512]{1,0:T(4,128)S(1)} %log_add_fusion, pred[512,512]{0,1:T(8,128)(4,1)S(1)} %iota_compare_fusion, f32[1,512,4,3,64]{1,4,3,2,0:T(8,128)S(1)} %bitcast.154), kind=kOutput, calls=%fused_computation.52 | convolution fusion | flops 138543104 | bytes 4988928 | tf_op jit(solution)/shard_map/shqk,skhe->sqhe/dot_general | solution.py:83
  99.4 3.0 %fusion.13 = f32[512,1024]{1,0:T(8,128)S(1)} fusion(bf16[512,1024]{1,0:T(8,128)(2,1)S(1)} %copy-done.19, bf16[1024,3072]{1,0:T(8,128)(2,1)} %bitcast.182), kind=kOutput, calls=%fused_computation.35 | convolution fusion | flops 1073741824 | bytes 5242880 | tf_op jit(solution)/shard_map/dot_general | solution.py:371
  102.4 1.5 add_convert_fusion.1
  104.0 1.4 add_convert_fusion.4
  105.4 1.5 copy.72
  106.9 3.3 %convolution_convert_fusion.2 = bf16[8,128,768]{2,1,0:T(8,128)(2,1)} fusion(bf16[8,128,512]{2,1,0:T(8,128)(2,1)S(1)} %bitcast.163, bf16[512,768,1]{0,1,2:T(8,128)(2,1)} %bitcast.168), kind=kOutput, calls=%fused_computation.39 | convolution fusion | flops 806092800 | bytes 3407872 | tf_op jit(solution)/shard_map/dot_general | solution.py:371
  110.2 1.5 copy.82
  112.2 2.3 %copy.99 = bf16[1024,512]{1,0:T(8,128)(2,1)} copy(bf16[1024,512]{0,1:T(8,128)(2,1)} %bitcast.157) | data formatting | bytes 2097152 | tf_op jit(solution)/shard_map/dot_general | solution.py:371
  114.5 2.9 %convolution_convert_fusion.1 = bf16[8,128,1024]{2,1,0:T(8,128)(2,1)S(1)} fusion(bf16[8,128,512]{2,1,0:T(8,128)(2,1)} %bitcast.164, bf16[512,1024]{1,0:T(8,128)(2,1)} %copy-done.21), kind=kOutput, calls=%fused_computation.30 | convolution fusion | flops 1074790400 | bytes 4194304 | tf_op jit(solution)/shard_map/dot_general | solution.py:371
  117.4 1.3 convolution_convert_fusion
  118.8 3.1 %pad_maximum_fusion.g_ref = bf16[8,128,3072]{2,1,0:T(8,128)(2,1)} fusion(bf16[8,128,1024]{2,1,0:T(8,128)(2,1)S(1)} %convolution_convert_fusion, bf16[8,128,1024]{2,1,0:T(8,128)(2,1)S(1)} %convolution_convert_fusion.1, bf16[8,128,256]{2,1,0:T(8,128)(2,1)S(1)} %convolution_convert_fusion.3, bf16[8,128,768]{2,1,0:T(8,128)(2,1)S(1)} %copy-done.7), kind=kLoop, calls=%fused_computation | loop fusion | flops 25165824 | bytes 12582912 | tf_op jit(solution)/shard_map/concatenate | solution.py:432
  122.0 54.3 %reduce_all.1 = (f32[128,3072]{1,0:T(8,128)S(1)}, f32[128,1024]{1,0:T(8,128)S(1)}, f32[128,1024]{1,0:T(8,128)S(1)}, f32[8,128]{1,0:T(8,128)S(1)}) custom-call(bf16[8,128,3072]{2,1,0:T(8,128)(2,1)} %pad_maximum_fusion.g_ref, bf16[4,128,1024]{2,1,0:T(8,128)(2,1)S(1)} %bitcast.148, bf16[4,128,1024]{2,1,0:T(8,128)(2,1)S(1)} %bitcast.149, ...), custom_call_target="tpu_custom_call" | custom-call | tf_op jit(solution)/shard_map/reduce_all/pallas_call | solution.py:300
  177.0 1.0 slice_bitcast_fusion
  178.1 2.0 %copy.90 = f32[1024,128]{1,0:T(8,128)} copy(f32[1024,128]{0,1:T(8,128)} %get-tuple-element.67) | data formatting | bytes 1048576
  (109 shorter events, 15.3 us)
Async XLA Ops:
  0.6 4.0 %copy-start.18 = (bf16[128]{0:T(256)(128)(2,1)S(1)}, bf16[128]{0:T(256)(128)(2,1)}, u32[]{:S(2)}) copy-start(bf16[128]{0:T(256)(128)(2,1)} %param.10) | copy-start | bytes 772
  0.6 4.0 %copy-start.17 = (bf16[256]{0:T(256)(128)(2,1)S(1)}, bf16[256]{0:T(256)(128)(2,1)}, u32[]{:S(2)}) copy-start(bf16[256]{0:T(256)(128)(2,1)} %param.11) | copy-start | bytes 1540
  58.2 4.8 %copy-start.4 = (bf16[4,128,1024]{2,1,0:T(8,128)(2,1)S(1)}, bf16[4,128,1024]{2,1,0:T(8,128)(2,1)}, u32[]{:S(2)}) copy-start(bf16[4,128,1024]{2,1,0:T(8,128)(2,1)} %get-tuple-element.16) | copy-start | bytes 3145732
  59.7 3.2 %copy-start.14 = (f32[4,128]{1,0:T(4,128)}, f32[4,128]{1,0:T(4,128)S(1)}, u32[]{:S(2)}) copy-start(f32[4,128]{1,0:T(4,128)S(1)} %get-tuple-element.96) | copy-start | bytes 6148
  63.0 5.3 %copy-start.13 = (f32[8,4,1,384]{3,1,2,0:T(4,128)}, f32[8,4,1,384]{3,1,2,0:T(4,128)S(1)}, u32[]{:S(2)}) copy-start(f32[8,4,1,384]{3,1,2,0:T(4,128)S(1)} %copy.120) | copy-start | bytes 147460
  71.6 7.6 %copy-start.3 = (f32[4,512,512]{1,2,0:T(8,128)}, f32[4,512,512]{1,2,0:T(8,128)S(1)}, u32[]{:S(2)}) copy-start(f32[4,512,512]{1,2,0:T(8,128)S(1)} %get-tuple-element.100) | copy-start | bytes 12582916
  71.6 2.0 %copy-start.8 = (bf16[4,128,1024]{2,1,0:T(8,128)(2,1)S(1)}, bf16[4,128,1024]{2,1,0:T(8,128)(2,1)}, u32[]{:S(2)}) copy-start(bf16[4,128,1024]{2,1,0:T(8,128)(2,1)} %get-tuple-element.19) | copy-start | bytes 3145732
  81.7 4.5 %copy-start.9 = (bf16[4,128,1024]{2,1,0:T(8,128)(2,1)S(1)}, bf16[4,128,1024]{2,1,0:T(8,128)(2,1)}, u32[]{:S(2)}) copy-start(bf16[4,128,1024]{2,1,0:T(8,128)(2,1)} %get-tuple-element.19) | copy-start | bytes 3145732
  81.7 9.3 %slice-start = ((s8[6291456]{0:T(1024)(128)(4,1)}), s8[4194304]{0:T(1024)(128)(4,1)S(1)}, s32[]{:S(2)}) async-start(s8[6291456]{0:T(1024)(128)(4,1)} %bitcast.184), calls=%async_computation | async-start | bytes 8388608
  86.2 4.8 %slice-start.1 = ((s8[6291456]{0:T(1024)(128)(4,1)}), s8[2097152]{0:T(1024)(128)(4,1)S(1)}, s32[]{:S(2)}) async-start(s8[6291456]{0:T(1024)(128)(4,1)} %bitcast.184), calls=%async_computation.1 | async-start | bytes 4194304
  90.0 1.0 copy-start.21
  91.0 1.3 copy-start.12
  92.3 3.4 %copy-start.6 = (bf16[1,128,1024]{2,1,0:T(8,128)(2,1)S(1)}, bf16[1,128,1024]{2,1,0:T(8,128)(2,1)}, u32[]{:S(2)}) copy-start(bf16[1,128,1024]{2,1,0:T(8,128)(2,1)} %param.9) | copy-start | bytes 786436
  95.9 3.5 %copy-start.19 = (bf16[512,1024]{1,0:T(8,128)(2,1)S(1)}, bf16[512,1024]{1,0:T(8,128)(2,1)}, u32[]{:S(2)}) copy-start(bf16[512,1024]{1,0:T(8,128)(2,1)} %get-tuple-element.97) | copy-start | bytes 3145732
  99.4 3.0 %copy-start.10 = (bf16[4,64,512]{2,1,0:T(8,128)(2,1)}, bf16[4,64,512]{2,1,0:T(8,128)(2,1)S(1)}, u32[]{:S(2)}) copy-start(bf16[4,64,512]{2,1,0:T(8,128)(2,1)S(1)} %convolution_convert_fusion.4) | copy-start | bytes 786436
  102.4 1.6 copy-start.15
  102.4 1.6 copy-start.16
  110.2 1.5 copy-start.11
  114.5 2.9 %copy-start.20 = (bf16[512,1024]{1,0:T(8,128)(2,1)S(1)}, bf16[512,1024]{1,0:T(8,128)(2,1)}, u32[]{:S(2)}) copy-start(bf16[512,1024]{1,0:T(8,128)(2,1)} %get-tuple-element.97) | copy-start | bytes 3145732
  117.4 1.4 copy-start.7
  118.8 3.1 %copy-start = (bf16[512,1024]{1,0:T(8,128)(2,1)S(1)}, bf16[512,1024]{1,0:T(8,128)(2,1)}, u32[]{:S(2)}) copy-start(bf16[512,1024]{1,0:T(8,128)(2,1)} %get-tuple-element.66) | copy-start | bytes 3145732
  176.2 0.8 copy-start.1
  177.0 3.1 %copy-start.5 = (bf16[1,128,1024]{2,1,0:T(8,128)(2,1)S(1)}, bf16[1,128,1024]{2,1,0:T(8,128)(2,1)}, u32[]{:S(2)}) copy-start(bf16[1,128,1024]{2,1,0:T(8,128)(2,1)} %param.8) | copy-start | bytes 786436
  177.0 4.4 %copy-start.2 = (f32[128,1024]{1,0:T(8,128)S(1)}, f32[128,1024]{1,0:T(8,128)}, u32[]{:S(2)}) copy-start(f32[128,1024]{1,0:T(8,128)} %copy-done.1) | copy-start | bytes 1572868

commit v2 on v0

v2 whole, which is shorter than its diff:
```python
import functools
import math

import jax
import jax.numpy as jnp
import numpy as np
from jax import lax
from jax.experimental import pallas as pl
from jax.experimental.pallas import tpu as pltpu
from jax.sharding import PartitionSpec as P

D = 1024
H = 16
HD = 64
FF = 4096
ROT = 16
LANES = 128

norm_eps = 1e-05
masked_score = -1e30
MESH = pl.DeviceIdType.MESH
f32, bf16 = jnp.float32, jnp.bfloat16


def rotary_tables(tok_len):
    half = ROT // 2
    frequency = np.power(np.float32(10000.0), np.float32(-2.0) * np.arange(half, dtype=np.float32) / np.float32(ROT))
    angles = np.arange(tok_len, dtype=np.float32)[:, None] * frequency.astype(np.float32)[None, :]
    cosine, sine = np.cos(angles.astype(np.float64)), np.sin(angles.astype(np.float64))
    keep = np.ones((tok_len, 2, 3, HD), np.float32)
    right = np.zeros((tok_len, 2, 3, HD), np.float32)
    left = np.zeros((tok_len, 2, 3, HD), np.float32)
    for part in range(2):
        keep[:, :, part, :half] = cosine[:, None]
        keep[:, :, part, half:ROT] = cosine[:, None]
        right[:, :, part, :half] = -sine[:, None]
        left[:, :, part, half:ROT] = sine[:, None]
    return [jnp.asarray(table.reshape(tok_len, 6 * HD)) for table in (keep, right, left)]


def mul(a, b, ca, cb):
    return lax.dot_general(a, b, (((ca,), (cb,)), ((), ())), preferred_element_type=f32)


def layer_kernel(
    chips, groups,
    w_ref, x_ref, c_ref, s_ref, keep_ref, right_ref, left_ref,
    lay_ref, gin_ref, g_out, v_out,
    w_all, x_all, c_all, s_all, normed, rows_a, rows_m, turned_a, turned_m, turned_c,
    q_s, k_s, v_s, probs, mixed_s, both_rows, slope, hid_grad, mg_s, dq_s, dk_s, dv_s, low_p, low_ds, tg,
    p_out, p_got, n_out, n_got, g, g_half, g_sum, g_got, v_mine, v_half, v_sum, v_got, v_all, v_last,
    local_sem, w_send, w_recv, h_send, h_recv, s_send, s_recv, z_send, z_recv,
    gh_send, gh_recv, ga_send, ga_recv, v_send, v_recv,
):
    length, tok_len = x_ref.shape[0], x_all.shape[0]
    depth = w_ref.shape[0]
    heads = H // groups
    in_width, out_width, up_width = 3 * D // groups, D // groups, FF // groups
    at_up, at_out = in_width, in_width + up_width
    at_down, width = at_out + out_width, at_out + out_width + up_width
    pieces = [(0, in_width), (at_up, up_width), (at_out, out_width + up_width)]
    norm_size, bias_size = 4 * D // (2 * chips * groups), (4 * D + FF) // (2 * chips * groups)

    dp, z = lax.axis_index("dp"), lax.axis_index("seq")
    chip, core = dp // 2, dp % 2
    partner = {"dp": chip * 2 + (1 - core)}
    across = [{"dp": (chip + k) % chips * 2 + core} for k in range(chips)]
    along = [{"seq": (z + k) % groups} for k in range(groups)]

    def block(at, size):
        return pl.ds(pl.multiple_of(at * size, size), size)

    def remote(source, target, send, recv, at, peer):
        return pltpu.make_async_remote_copy(
            src_ref=source, dst_ref=target, send_sem=send.at[at], recv_sem=recv.at[at],
            device_id=peer, device_id_type=MESH,
        )

    started = []

    def send(*args):
        copy = remote(*args)
        copy.start()
        started.append(copy)
        return copy

    own_rows, own_toks = block(dp, depth), block(z, length)
    local = [
        pltpu.make_async_copy(w_ref, w_all.at[own_rows], local_sem.at[0]),
        pltpu.make_async_copy(x_ref, x_all.at[own_toks], local_sem.at[1]),
        pltpu.make_async_copy(c_ref, c_all.at[own_toks], local_sem.at[2]),
        pltpu.make_async_copy(s_ref, s_all.at[dp, z], local_sem.at[3]),
    ]
    for copy in local:
        copy.start()
    barrier = pltpu.get_barrier_semaphore()
    peers = [partner] + across[1:] + along[1:]
    for peer in peers:
        pl.semaphore_signal(barrier, inc=1, device_id=peer, device_id_type=MESH)
    pl.semaphore_wait(barrier, len(peers))

    smalls = [send(s_ref, s_all.at[dp, z], z_send, z_recv, (0, k), along[k]) for k in range(1, groups)]
    weights, handed = {}, {}

    def send_piece(at):
        cols = pl.ds(*pieces[at])
        for k in range(1, chips):
            weights[at, k] = send(
                w_ref.at[:, cols], w_all.at[own_rows, cols], w_send, w_recv, (at, k), across[k]
            )
        handed[at] = [
            send(w_ref.at[:, cols], w_all.at[own_rows, cols], h_send, h_recv, (at, 0), partner)
        ]

    def take_piece(at):
        cols = pl.ds(*pieces[at])
        for k in range(1, chips):
            weights[at, k].wait_recv()
            came = block((chip + chips - k) % chips * 2 + core, depth)
            handed[at].append(
                send(w_all.at[came, cols], w_all.at[came, cols], h_send, h_recv, (at, k), partner)
            )
        for copy in handed[at]:
            copy.wait_recv()

    send_piece(0)
    x_moves = [send(x_ref, x_all.at[own_toks], z_send, z_recv, (1, k), along[k]) for k in range(1, groups)]
    send_piece(1)
    send_piece(2)
    c_moves = [send(c_ref, c_all.at[own_toks], z_send, z_recv, (2, k), along[k]) for k in range(1, groups)]

    local[3].wait()
    for copy in smalls:
        copy.wait_recv()
    out = [send(s_all.at[dp], s_all.at[dp], s_send, s_recv, (0, k), across[k]) for k in range(1, chips)]
    over = [send(s_all.at[dp], s_all.at[dp], s_send, s_recv, (1, 0), partner)]
    for k in range(1, chips):
        out[k - 1].wait_recv()
        came = (chip + chips - k) % chips * 2 + core
        over.append(send(s_all.at[came], s_all.at[came], s_send, s_recv, (1, k), partner))
    for copy in over:
        copy.wait_recv()
    for copy in x_moves:
        copy.wait_recv()
    local[1].wait()

    def owners(size, base, step, row, first):
        per, share = max(size // LANES, 1), max(LANES // size, 1)
        at = base // per * share + z * (step // per * share) + row // per * share
        return [((at + j) // groups, (at + j) % groups, first + row % per) for j in range(share)]

    def small_vector(size, base, step, count, first):
        parts = []
        for row in range(count):
            total = None
            for d_at, z_at, line in owners(size, base, step, row, first):
                value = s_all[d_at, z_at][line : line + 1, :]
                total = value if total is None else total + value
            parts.append(total)
        return jnp.concatenate(parts, axis=1)

    norm_vec = [small_vector(norm_size, r * (D // LANES), 0, D // LANES, 0) for r in range(4)]

    def normalise(values):
        centered = values - jnp.mean(values, axis=-1, keepdims=True)
        inv_std = lax.rsqrt(jnp.mean(centered * centered, axis=-1, keepdims=True) + norm_eps)
        return centered * inv_std, inv_std

    def norm_step(i, carry):
        at = block(i, length)
        part, _ = normalise(x_all[at, :].astype(f32))
        normed[at, :] = part
        a_part = part * norm_vec[0] + norm_vec[1]
        m_part = part * norm_vec[2] + norm_vec[3]
        rows_a[at, :] = a_part.astype(bf16)
        rows_m[at, :] = m_part.astype(bf16)
        turned_a[:, at] = a_part.T.astype(bf16)
        turned_m[:, at] = m_part.T.astype(bf16)
        return carry

    lax.fori_loop(0, groups, norm_step, 0)

    in_bias = small_vector(bias_size, 0, in_width // LANES, in_width // LANES, 1)
    local[0].wait()
    take_piece(0)
    pair = 6 * HD

    def turn(values, sign):
        return (
            values * keep_ref[...]
            + sign * (pltpu.roll(values, pair - ROT // 2, 1) * right_ref[...])
            + sign * (pltpu.roll(values, ROT // 2, 1) * left_ref[...])
        )

    for two in range(heads // 2):
        cols = slice(two * pair, (two + 1) * pair)
        triple = mul(rows_a[...], w_all[:, cols], 1, 0) + in_bias[:, cols]
        triple = turn(triple, 1.0)
        for j in range(2):
            h = two * 2 + j
            q_s[h] = triple[:, j * 192 : j * 192 + 64].astype(bf16)
            k_s[h] = triple[:, j * 192 + 64 : j * 192 + 128].astype(bf16)
            v_s[h] = triple[:, j * 192 + 128 : j * 192 + 192].astype(bf16)

    step_rows = 128
    scale = HD ** (-0.5)

    def attend(h):
        for b in range(tok_len // step_rows):
            at, seen = slice(b * step_rows, (b + 1) * step_rows), (b + 1) * step_rows
            scores = mul(q_s[h, at, :], k_s[h, :seen, :], 1, 1) * scale
            q_pos = lax.broadcasted_iota(jnp.int32, scores.shape, 0) + b * step_rows
            k_pos = lax.broadcasted_iota(jnp.int32, scores.shape, 1)
            scores = jnp.where(q_pos >= k_pos, scores, masked_score)
            row_max = jnp.max(scores, axis=-1, keepdims=True)
            powers = jnp.exp(scores - row_max)
            part = powers * (1.0 / jnp.sum(powers, axis=-1, keepdims=True))
            probs[h, at, :seen] = part
            mixed_s[h, at, :] = mul(part.astype(bf16), v_s[h, :seen, :], 1, 0)

    for h in range(heads):
        attend(h)
    both_rows[:, :out_width] = jnp.concatenate([mixed_s[h] for h in range(heads)], axis=1).astype(bf16)

    up_bias = small_vector(bias_size, 3 * D // LANES, up_width // LANES, up_width // LANES, 1)
    take_piece(1)
    wide = 256
    for j in range(up_width // wide):
        cols = slice(j * wide, (j + 1) * wide)
        up_cols = slice(at_up + j * wide, at_up + (j + 1) * wide)
        hidden = mul(rows_m[...], w_all[:, up_cols], 1, 0) + up_bias[:, cols]
        half = 0.5 * (1.0 + lax.erf(hidden * (1.0 / math.sqrt(2.0))))
        both_rows[:, out_width + j * wide : out_width + (j + 1) * wide] = (hidden * half).astype(bf16)
        slope[:, cols] = half + hidden * jnp.exp(-0.5 * hidden * hidden) * (1.0 / math.sqrt(2.0 * math.pi))

    take_piece(2)
    p_moves = []
    for k in list(range(1, groups)) + [0]:
        at = block((z + k) % groups, length)
        part = mul(both_rows[at, :], w_all[:, at_out:], 1, 1)
        p_out[k] = part.astype(bf16)
        if k > 0:
            p_moves.append(send(p_out.at[k], p_got.at[k], z_send, z_recv, (3, k), along[k]))

    for copy in c_moves:
        copy.wait_recv()
    local[2].wait()

    def turn_cot(i, carry):
        at = block(i, length)
        turned_c[:, at] = c_all[at, :].astype(f32).T.astype(bf16)
        return carry

    lax.fori_loop(0, groups, turn_cot, 0)
    halves, sums = {}, []
    order = list(range(1, chips)) + [0]

    def give(at):
        cols = pl.ds(*pieces[at])
        for k in order:
            rows = block((chip + k) % chips * 2 + 1 - core, depth)
            halves[at, k] = send(
                g.at[rows, cols], g_half.at[k, :, cols], gh_send, gh_recv, (at, k), partner
            )

    def add(at):
        cols = pl.ds(*pieces[at])
        for k in order:
            rows = block((chip + k) % chips * 2 + core, depth)
            halves[at, k].wait_recv()
            both = g[rows, cols].astype(f32) + g_half[k, :, cols].astype(f32)
            if k > 0:
                g_sum[k, :, cols] = both.astype(bf16)
                sums.append(
                    send(g_sum.at[k, :, cols], g_got.at[k, :, cols], ga_send, ga_recv, (at, k), across[k])
                )
            else:
                g_out[:, cols] = both

    for j in range((out_width + up_width) // wide):
        cols = slice(j * wide, (j + 1) * wide)
        g[:, at_out + j * wide : at_out + (j + 1) * wide] = mul(turned_c[...], both_rows[:, cols], 1, 0).astype(bf16)
    give(2)

    up_sums = []
    for j in range(up_width // wide):
        cols = slice(j * wide, (j + 1) * wide)
        part = mul(c_all[...], w_all[:, at_down + j * wide : at_down + (j + 1) * wide], 1, 0) * slope[:, cols]
        part = part.astype(bf16)
        hid_grad[:, cols] = part
        up_sums.append(jnp.sum(part.astype(f32), axis=0, keepdims=True))
    add(2)
    for j in range(up_width // wide):
        cols = slice(j * wide, (j + 1) * wide)
        g[:, at_up + j * wide : at_up + (j + 1) * wide] = mul(turned_m[...], hid_grad[:, cols], 1, 0).astype(bf16)
    give(1)

    mixed_grad = mul(c_all[...], w_all[:, at_out:at_down], 1, 0).astype(bf16)
    for h in range(heads):
        mg_s[h] = mixed_grad[:, h * HD : (h + 1) * HD]
    add(1)

    def attend_back(h):
        for b in range(tok_len // step_rows):
            at, seen = slice(b * step_rows, (b + 1) * step_rows), (b + 1) * step_rows
            part, m_grad = probs[h, at, :seen], mg_s[h, at, :]
            p_grad = mul(m_grad, v_s[h, :seen, :], 1, 1)
            row_dot = jnp.sum(part * p_grad, axis=-1, keepdims=True)
            s_grad = (part * (p_grad - row_dot)).astype(bf16)
            dq_s[h, at, :] = mul(s_grad, k_s[h, :seen, :], 1, 0) * scale
            low_p[at, :seen] = part.astype(bf16)
            low_ds[at, :seen] = s_grad
        for b in range(tok_len // step_rows):
            at, late = slice(b * step_rows, (b + 1) * step_rows), slice(b * step_rows, tok_len)
            dk_s[h, at, :] = mul(low_ds[late, at], q_s[h, late, :], 0, 0) * scale
            dv_s[h, at, :] = mul(low_p[late, at], mg_s[h, late, :], 0, 0)

    for h in range(heads):
        attend_back(h)
    in_sums = []
    for two in range(heads // 2):
        joined = []
        for h in (two * 2, two * 2 + 1):
            joined += [dq_s[h], dk_s[h], dv_s[h]]
        part = turn(jnp.concatenate(joined, axis=1), -1.0).astype(bf16)
        tg[:, two * pair : (two + 1) * pair] = part
        in_sums.append(jnp.sum(part.astype(f32), axis=0, keepdims=True))

    norm_sums = None
    n_moves = []
    for k in list(range(1, groups)) + [0]:
        at = block((z + k) % groups, length)
        a_grad = mul(tg[at, :], w_all[:, :in_width], 1, 1)
        m_grad = mul(hid_grad[at, :], w_all[:, at_up:at_out], 1, 1)
        n_out[k] = (a_grad * norm_vec[0] + m_grad * norm_vec[2]).astype(bf16)
        if k > 0:
            n_moves.append(send(n_out.at[k], n_got.at[k], z_send, z_recv, (4, k), along[k]))
        part = normed[at, :]
        terms = [a_grad * part, a_grad, m_grad * part, m_grad]
        terms = [jnp.sum(term, axis=0, keepdims=True) for term in terms]
        norm_sums = terms if norm_sums is None else [a + b for a, b in zip(norm_sums, terms)]

    for j in range(in_width // wide):
        cols = slice(j * wide, (j + 1) * wide)
        g[:, cols] = mul(turned_a[...], tg[:, cols], 1, 0).astype(bf16)
    give(0)

    v_mine[...] = jnp.zeros_like(v_mine)

    def place(vector, size, base, step, first):
        for row in range(vector.shape[1] // LANES):
            for d_at, z_at, line in owners(size, base, step, row, first):
                v_mine[d_at, z_at, line : line + 1, :] = vector[:, row * LANES : (row + 1) * LANES]

    for r in range(4):
        place(norm_sums[r], norm_size, r * (D // LANES), 0, 0)
    place(jnp.concatenate(in_sums, axis=1), bias_size, 0, in_width // LANES, 1)
    place(jnp.concatenate(up_sums, axis=1), bias_size, 3 * D // LANES, up_width // LANES, 1)
    cot_own = c_ref[...].astype(f32)
    place(jnp.sum(cot_own, axis=0, keepdims=True), bias_size, (3 * D + FF) // LANES, 0, 1)
    v_give = [
        send(v_mine.at[(chip + k) % chips * 2 + 1 - core], v_half.at[k], v_send, v_recv, (0, k), partner)
        for k in range(chips)
    ]
    add(0)
    v_across = []
    for k in order:
        v_give[k].wait_recv()
        v_sum[k] = v_mine[(chip + k) % chips * 2 + core] + v_half[k]
        if k > 0:
            v_across.append(send(v_sum.at[k], v_got.at[k], v_send, v_recv, (1, k), across[k]))

    for copy in p_moves:
        copy.wait_recv()
    out_bias = small_vector(bias_size, (3 * D + FF) // LANES, 0, D // LANES, 1)
    own = x_ref[...].astype(f32)
    total = p_out[0].astype(f32)
    for k in range(1, groups):
        total = total + p_got[k].astype(f32)
    lay_ref[...] = (own + total + out_bias).astype(bf16)

    total = v_sum[0]
    for copy in v_across:
        copy.wait_recv()
    for k in range(1, chips):
        total = total + v_got[k]
    v_all[...] = total
    v_along = [
        send(v_all.at[(z + k) % groups], v_last.at[k], z_send, z_recv, (5, k), along[k])
        for k in range(1, groups)
    ]

    for copy in n_moves:
        copy.wait_recv()
    own_normed, own_std = normalise(own)
    total = n_out[0].astype(f32)
    for k in range(1, groups):
        total = total + n_got[k].astype(f32)
    term = own_std * (
        total
        - jnp.mean(total, axis=-1, keepdims=True)
        - own_normed * jnp.mean(total * own_normed, axis=-1, keepdims=True)
    )
    gin_ref[...] = (cot_own + term).astype(bf16)

    for copy in v_along:
        copy.wait_recv()
    total = v_all[z]
    for k in range(1, groups):
        total = total + v_last[k]
    v_out[...] = total

    for copy in sums:
        copy.wait_recv()
    total = g_out[...]
    for k in range(1, chips):
        total = total + g_got[k].astype(f32)
    g_out[...] = total
    for copy in started:
        copy.wait_send()


def layer(w, x, c, s, tables, chips, groups):
    vm = pl.BlockSpec(memory_space=pltpu.VMEM)
    dma = pltpu.SemaphoreType.DMA
    length, depth, width = x.shape[0], w.shape[0], w.shape[1]
    tok_len, devices, heads = length * groups, 2 * chips, H // groups
    up_width, in_width = FF // groups, 3 * D // groups
    shape, rows, head = (tok_len, D), (groups, length, D), (heads, tok_len, HD)
    tile = (8, LANES)
    buffers = [
        ((D, width), bf16), (shape, bf16), (shape, bf16), ((devices, groups) + tile, f32),
        (shape, f32), (shape, bf16), (shape, bf16),
        ((D, tok_len), bf16), ((D, tok_len), bf16), ((D, tok_len), bf16),
        (head, bf16), (head, bf16), (head, bf16), ((heads, tok_len, tok_len), f32), (head, f32),
        ((tok_len, heads * HD + up_width), bf16), ((tok_len, up_width), f32),
        ((tok_len, up_width), bf16), (head, bf16), (head, f32), (head, f32), (head, f32),
        ((tok_len, tok_len), bf16), ((tok_len, tok_len), bf16),
        ((tok_len, in_width), bf16),
        (rows, bf16), (rows, bf16), (rows, bf16), (rows, bf16),
        ((D, width), bf16), ((chips, depth, width), bf16), ((chips, depth, width), bf16),
        ((chips, depth, width), bf16),
        ((devices, groups) + tile, f32), ((chips, groups) + tile, f32), ((chips, groups) + tile, f32),
        ((chips, groups) + tile, f32), ((groups,) + tile, f32), ((groups,) + tile, f32),
    ]
    sems = [(4,)] + [(3, chips)] * 4 + [(2, chips)] * 2 + [(6, groups)] * 2 + [(3, chips)] * 4 + [(2, chips)] * 2
    return pl.pallas_call(
        functools.partial(layer_kernel, chips, groups),
        out_shape=(
            jax.ShapeDtypeStruct(x.shape, bf16),
            jax.ShapeDtypeStruct(x.shape, bf16),
            jax.ShapeDtypeStruct(w.shape, f32),
            jax.ShapeDtypeStruct(tile, f32),
        ),
        in_specs=[vm] * 7,
        out_specs=(vm,) * 4,
        scratch_shapes=[pltpu.VMEM(*buffer) for buffer in buffers] + [dma(sem) for sem in sems],
        compiler_params=pltpu.CompilerParams(
            collective_id=0, has_side_effects=True, vmem_limit_bytes=60 * 2**20
        ),
        name="layer",
    )(w, x, c, s, *tables)


def body(hidden_in, out_grad, norm_params, biases, attn_in, attn_out, mlp_up, mlp_down):
    groups, devices = lax.axis_size("seq"), lax.axis_size("dp")
    chips = devices // 2
    length = hidden_in.shape[1]
    in_width, out_width, up_width = attn_in.shape[1], attn_out.shape[0], mlp_up.shape[1]
    norm_size, bias_size = norm_params.shape[0], biases.shape[0]
    flat = lax.axis_index("dp") * groups + lax.axis_index("seq")

    def tile_rows(values):
        size = values.shape[0]
        if size >= LANES:
            return values.reshape(size // LANES, LANES)
        offset = flat % (LANES // size) * size
        return lax.dynamic_update_slice(jnp.zeros((LANES,), values.dtype), values, (offset,))[None]

    def from_rows(rows, size):
        if size >= LANES:
            return rows.reshape(size)
        return lax.dynamic_slice(rows.reshape(LANES), (flat % (LANES // size) * size,), (size,))

    small = jnp.concatenate([tile_rows(norm_params.astype(f32)), tile_rows(biases.astype(f32))], axis=0)
    norm_lines, lines = max(norm_size // LANES, 1), small.shape[0]
    small = jnp.pad(small, ((0, 8 - lines), (0, 0)))
    packed = jnp.concatenate([attn_in, mlp_up, attn_out.T, mlp_down.T], axis=1)
    layer_out, grad_input, grads, sums = layer(
        packed, hidden_in[0], out_grad[0], small, rotary_tables(length * groups), chips, groups
    )
    at_out = in_width + up_width
    return (
        layer_out[None],
        grad_input[None],
        from_rows(sums[:norm_lines], norm_size),
        from_rows(sums[norm_lines:lines], bias_size),
        grads[:, :in_width],
        grads[:, at_out : at_out + out_width].T,
        grads[:, in_width:at_out],
        grads[:, at_out + out_width :].T,
    )


def solution(mesh):
    in_specs = (
        P("dp", "seq", None),
        P("dp", "seq", None),
        P(("dp", "seq")),
        P(("dp", "seq")),
        P("dp", "seq"),
        P("seq", "dp"),
        P("dp", "seq"),
        P("seq", "dp"),
    )
    out_specs = (
        P("dp", "seq", None),
        P("dp", "seq", None),
        P(("dp", "seq")),
        P(("dp", "seq")),
        P("dp", "seq"),
        P("seq", "dp"),
        P("dp", "seq"),
        P("seq", "dp"),
    )
    return jax.shard_map(body, mesh=mesh, in_specs=in_specs, out_specs=out_specs, check_vma=False)
```

time: 568 us -> 129 us (0.23)
  waiting for transfers between devices: 307 us -> 0 us
  blocking collectives: 182 us -> 0 us
  Pallas kernels: 0 us -> 113 us
  matrix products: 41.9 us -> 0 us
  between operations: 14.4 us -> 0.67 us
  other arithmetic: 11.1 us -> 3.26 us
    reduce_scatter x7 -> x0, waiting for transfers between devices: 263 us -> none  [the longest x1 55.6 us: body(): lax.psum_scatter(down_term, 'dp', scatter_dimension=1, tiled=True)]
    all_gather x3 -> x0, blocking collectives: 142 us -> none  [the longest x1 69.7 us: body(): lax.all_gather(norm_params, ('dp', 'seq'), axis=0, tiled=True)]
    pallas_call x0 -> x1, Pallas kernels: none -> 113 us  [layer(): pl.pallas_call(functools.partial(layer_kernel, chips, groups), out_shape=...]
    dot_general x18 -> x0, matrix products: 41.9 us -> none  [the longest x1 4.95 us: body(): jnp.dot(up_rows, w_up, preferred_element_type=jnp.float32) + up_bias_vec]
    all_gather x6 -> x0, waiting for transfers between devices: 40.9 us -> none  [the longest x1 25 us: body(): lax.all_gather(pieces[3], 'dp', axis=1, tiled=True)]
    unnamed x1 -> x0, blocking collectives: 40 us -> none
    reduce_sum x6 -> x0, other arithmetic: 7.36 us -> none  [the longest x1 2.49 us: body(): shift_attn = jnp.sum(attn_grad_rows, axis=0)]
  transfers between devices with their start and end apart: 13 -> 0, of which waited for: 8 -> 0; matrix products, arithmetic and copies ran while one was open for 10% -> 0% of each run, Pallas kernels for 0% -> 0%
where the time goes in v2:
time: 129 us
  Pallas kernels  113 us (88%)
  local copies, waits for them, and re-layouts  12.4 us (10%)
  other arithmetic  3.26 us (3%)
    pallas_call x1, Pallas kernels, layer(): pl.pallas_call(functools.partial(layer_kernel, chips, groups), out_shape=...  113 us
    unnamed x10, local copies, waits for them, and re-layouts  5.19 us

profile of v2, /device:TPU:0, one launch (start us, length us, event | category | flops | bytes accessed | tf_op | source)
XLA Modules:
  0.0 129.1 jit_solution(17339199187898594746)
XLA Ops:
  0.6 1.3 fusion.3.s_ref
  1.9 0.9 copy.19
  2.8 1.1 copy.20
  3.9 2.0 %pad_maximum_fusion.w_ref = bf16[128,3072]{1,0:T(8,128)(2,1)} fusion(bf16[128,1024]{1,0:T(8,128)(2,1)S(1)} %bitcast.16, bf16[128,256]{1,0:T(8,128)(2,1)S(1)} %bitcast.19, bf16[128,1024]{1,0:T(8,128)(2,1)} %param.17, bf16[128,768]{1,0:T(8,128)(2,1)} %param.15), kind=kLoop, calls=%fused_computation | loop fusion | flops 3145728 | bytes 1572864 | tf_op jit(solution)/shard_map/concatenate | solution.py:488
  5.9 112.7 %layer.1 = (bf16[128,1024]{1,0:T(8,128)(2,1)}, bf16[128,1024]{1,0:T(8,128)(2,1)}, f32[128,3072]{1,0:T(8,128)}, f32[8,128]{1,0:T(8,128)}) custom-call(bf16[128,3072]{1,0:T(8,128)(2,1)} %pad_maximum_fusion.w_ref, bf16[128,1024]{1,0:T(8,128)(2,1)} %bitcast.17, bf16[128,1024]{1,0:T(8,128)(2,1)} %bitcast.18, f32[8,128]{1,0:T(8,128)} %fusion.3.s_ref, ...), custom_call_target="tpu_custom_call" | custom-call | tf_op jit(solution)/shard_map/layer/pallas_call | solution.py:447
  118.7 1.2 slice_bitcast_fusion.3
  119.8 1.2 slice_bitcast_fusion.2
  121.1 0.9 slice_bitcast_fusion.1
  122.0 0.8 copy.21
  122.8 1.8 %slice.20 = f32[128,768]{1,0:T(8,128)} slice(f32[128,3072]{1,0:T(8,128)} %get-tuple-element.15), slice={[0:128], [0:768]} | slice | bytes 786432 | tf_op jit(solution)/shard_map/slice | solution.py:498
  124.5 0.0 copy-start.1
  124.5 0.0 copy-start
  124.5 2.1 %slice_bitcast_fusion = (f32[1024,128]{0,1:T(8,128)S(1)}, f32[128,1024]{1,0:T(8,128)}) fusion(f32[128,3072]{1,0:T(8,128)} %get-tuple-element.15), kind=kLoop, calls=%fused_computation.1 | loop fusion | bytes 2097152 | tf_op jit(solution)/shard_map/transpose | solution.py:501
  126.7 1.0 copy.22
  127.7 0.0 copy-done.1
  127.7 0.7 copy.25
  128.4 0.0 copy-done
  128.4 0.7 copy.26
Async XLA Ops:
  124.5 3.1 %copy-start.1 = (bf16[128,1024]{1,0:T(8,128)(2,1)S(1)}, bf16[128,1024]{1,0:T(8,128)(2,1)}, u32[]{:S(2)}) copy-start(bf16[128,1024]{1,0:T(8,128)(2,1)} %get-tuple-element.12) | copy-start | bytes 786436
  124.5 3.8 %copy-start = (bf16[128,1024]{1,0:T(8,128)(2,1)S(1)}, bf16[128,1024]{1,0:T(8,128)(2,1)}, u32[]{:S(2)}) copy-start(bf16[128,1024]{1,0:T(8,128)(2,1)} %get-tuple-element.13) | copy-start | bytes 786436

commit v3 on v2

--- a/solution.py
+++ b/solution.py
@@ -44,16 +44,16 @@
 
 def layer_kernel(
     chips, groups,
-    w_ref, x_ref, c_ref, s_ref, keep_ref, right_ref, left_ref,
-    lay_ref, gin_ref, g_out, v_out,
+    win_ref, wout_ref, wup_ref, wdown_ref, x_ref, c_ref, nrm_ref, bias_ref, keep_ref, right_ref, left_ref,
+    lay_ref, gin_ref, gi_ref, go_ref, gu_ref, gd_ref, v_out,
     w_all, x_all, c_all, s_all, normed, rows_a, rows_m, turned_a, turned_m, turned_c,
     q_s, k_s, v_s, probs, mixed_s, both_rows, slope, hid_grad, mg_s, dq_s, dk_s, dv_s, low_p, low_ds, tg,
     p_out, p_got, n_out, n_got, g, g_half, g_sum, g_got, v_mine, v_half, v_sum, v_got, v_all, v_last,
-    local_sem, w_send, w_recv, h_send, h_recv, s_send, s_recv, z_send, z_recv,
+    g_out, s_mine, w_send, w_recv, h_send, h_recv, s_send, s_recv, z_send, z_recv, x_send, x_recv,
     gh_send, gh_recv, ga_send, ga_recv, v_send, v_recv,
 ):
     length, tok_len = x_ref.shape[0], x_all.shape[0]
-    depth = w_ref.shape[0]
+    depth = win_ref.shape[0]
     heads = H // groups
     in_width, out_width, up_width = 3 * D // groups, D // groups, FF // groups
     at_up, at_out = in_width, in_width + up_width
@@ -85,31 +85,33 @@
         return copy
 
     own_rows, own_toks = block(dp, depth), block(z, length)
-    local = [
-        pltpu.make_async_copy(w_ref, w_all.at[own_rows], local_sem.at[0]),
-        pltpu.make_async_copy(x_ref, x_all.at[own_toks], local_sem.at[1]),
-        pltpu.make_async_copy(c_ref, c_all.at[own_toks], local_sem.at[2]),
-        pltpu.make_async_copy(s_ref, s_all.at[dp, z], local_sem.at[3]),
-    ]
-    for copy in local:
-        copy.start()
     barrier = pltpu.get_barrier_semaphore()
     peers = [partner] + across[1:] + along[1:]
     for peer in peers:
         pl.semaphore_signal(barrier, inc=1, device_id=peer, device_id_type=MESH)
+    w_all[own_rows, :in_width] = win_ref[...]
+    w_all[own_rows, at_up:at_out] = wup_ref[...]
+    w_all[own_rows, at_out:at_down] = wout_ref[...].astype(f32).T.astype(bf16)
+    w_all[own_rows, at_down:] = wdown_ref[...].astype(f32).T.astype(bf16)
+    x_all[own_toks, :] = x_ref[...]
+    c_all[own_toks, :] = c_ref[...]
+    s_mine[...] = jnp.zeros_like(s_mine)
+    s_mine[: nrm_ref.shape[0], :] = nrm_ref[...].astype(f32)
+    s_mine[nrm_ref.shape[0] : nrm_ref.shape[0] + bias_ref.shape[0], :] = bias_ref[...].astype(f32)
+    s_all[dp, z] = s_mine[...]
     pl.semaphore_wait(barrier, len(peers))
 
-    smalls = [send(s_ref, s_all.at[dp, z], z_send, z_recv, (0, k), along[k]) for k in range(1, groups)]
+    smalls = [send(s_mine, s_all.at[dp, z], z_send, z_recv, (0, k), along[k]) for k in range(1, groups)]
     weights, handed = {}, {}
 
     def send_piece(at):
         cols = pl.ds(*pieces[at])
         for k in range(1, chips):
             weights[at, k] = send(
-                w_ref.at[:, cols], w_all.at[own_rows, cols], w_send, w_recv, (at, k), across[k]
+                w_all.at[own_rows, cols], w_all.at[own_rows, cols], w_send, w_recv, (at, k), across[k]
             )
         handed[at] = [
-            send(w_ref.at[:, cols], w_all.at[own_rows, cols], h_send, h_recv, (at, 0), partner)
+            send(w_all.at[own_rows, cols], w_all.at[own_rows, cols], h_send, h_recv, (at, 0), partner)
         ]
 
     def take_piece(at):
@@ -123,13 +125,29 @@
         for copy in handed[at]:
             copy.wait_recv()
 
+    ways = [(-1, (z + 1) % groups, z < groups - 1), (1, (z + groups - 1) % groups, z > 0)]
+
+    def row_copy(way, j):
+        sign, to, _ = ways[way]
+        at = block((z + groups + sign * j) % groups, length)
+        return remote(x_all.at[at], x_all.at[at], x_send, x_recv, (way, j), {"seq": to})
+
+    def holds(way, j):
+        return z >= j if way == 0 else z + j < groups
+
+    def pass_rows(j):
+        for way in range(2):
+            if j > 0:
+                @pl.when(holds(way, j))
+                def _():
+                    row_copy(way, j - 1).wait_recv()
+            if j < groups - 1:
+                @pl.when(holds(way, j) & ways[way][2])
+                def _():
+                    row_copy(way, j).start()
+
     send_piece(0)
-    x_moves = [send(x_ref, x_all.at[own_toks], z_send, z_recv, (1, k), along[k]) for k in range(1, groups)]
-    send_piece(1)
-    send_piece(2)
-    c_moves = [send(c_ref, c_all.at[own_toks], z_send, z_recv, (2, k), along[k]) for k in range(1, groups)]
-
-    local[3].wait()
+    pass_rows(0)
     for copy in smalls:
         copy.wait_recv()
     out = [send(s_all.at[dp], s_all.at[dp], s_send, s_recv, (0, k), across[k]) for k in range(1, chips)]
@@ -140,9 +158,6 @@
         over.append(send(s_all.at[came], s_all.at[came], s_send, s_recv, (1, k), partner))
     for copy in over:
         copy.wait_recv()
-    for copy in x_moves:
-        copy.wait_recv()
-    local[1].wait()
 
     def owners(size, base, step, row, first):
         per, share = max(size // LANES, 1), max(LANES // size, 1)
@@ -166,7 +181,7 @@
         inv_std = lax.rsqrt(jnp.mean(centered * centered, axis=-1, keepdims=True) + norm_eps)
         return centered * inv_std, inv_std
 
-    def norm_step(i, carry):
+    def norm_step(i):
         at = block(i, length)
         part, _ = normalise(x_all[at, :].astype(f32))
         normed[at, :] = part
@@ -176,13 +191,24 @@
         rows_m[at, :] = m_part.astype(bf16)
         turned_a[:, at] = a_part.T.astype(bf16)
         turned_m[:, at] = m_part.T.astype(bf16)
-        return carry
-
-    lax.fori_loop(0, groups, norm_step, 0)
+
+    norm_step(z)
+    for j in range(1, groups):
+        pass_rows(j)
+        if j == 2:
+            take_piece(0)
+            send_piece(1)
+        if j == groups - 1:
+            send_piece(2)
+            c_moves = [
+                send(c_ref, c_all.at[own_toks], z_send, z_recv, (2, k), along[k]) for k in range(1, groups)
+            ]
+        for way in range(2):
+            @pl.when(holds(way, j))
+            def _():
+                norm_step((z + groups + ways[way][0] * j) % groups)
 
     in_bias = small_vector(bias_size, 0, in_width // LANES, in_width // LANES, 1)
-    local[0].wait()
-    take_piece(0)
     pair = 6 * HD
 
     def turn(values, sign):
@@ -216,11 +242,11 @@
             powers = jnp.exp(scores - row_max)
             part = powers * (1.0 / jnp.sum(powers, axis=-1, keepdims=True))
             probs[h, at, :seen] = part
-            mixed_s[h, at, :] = mul(part.astype(bf16), v_s[h, :seen, :], 1, 0)
+            mixed_s[h, at, :] = mul(part.astype(bf16), v_s[h, :seen, :], 1, 0).astype(bf16)
 
     for h in range(heads):
         attend(h)
-    both_rows[:, :out_width] = jnp.concatenate([mixed_s[h] for h in range(heads)], axis=1).astype(bf16)
+    both_rows[:, :out_width] = jnp.concatenate([mixed_s[h].astype(f32) for h in range(heads)], axis=1).astype(bf16)
 
     up_bias = small_vector(bias_size, 3 * D // LANES, up_width // LANES, up_width // LANES, 1)
     take_piece(1)
@@ -240,11 +266,10 @@
         part = mul(both_rows[at, :], w_all[:, at_out:], 1, 1)
         p_out[k] = part.astype(bf16)
         if k > 0:
-            p_moves.append(send(p_out.at[k], p_got.at[k], z_send, z_recv, (3, k), along[k]))
+            p_moves.append(send(p_out.at[k], p_got.at[k - 1], z_send, z_recv, (3, k), along[k]))
 
     for copy in c_moves:
         copy.wait_recv()
-    local[2].wait()
 
     def turn_cot(i, carry):
         at = block(i, length)
@@ -252,7 +277,7 @@
         return carry
 
     lax.fori_loop(0, groups, turn_cot, 0)
-    halves, sums = {}, []
+    halves, sums = {}, {}
     order = list(range(1, chips)) + [0]
 
     def give(at):
@@ -270,12 +295,26 @@
             halves[at, k].wait_recv()
             both = g[rows, cols].astype(f32) + g_half[k, :, cols].astype(f32)
             if k > 0:
-                g_sum[k, :, cols] = both.astype(bf16)
-                sums.append(
-                    send(g_sum.at[k, :, cols], g_got.at[k, :, cols], ga_send, ga_recv, (at, k), across[k])
+                g_sum[k - 1, :, cols] = both.astype(bf16)
+                sums[at, k] = send(
+                    g_sum.at[k - 1, :, cols], g_got.at[k - 1, :, cols], ga_send, ga_recv, (at, k), across[k]
                 )
             else:
                 g_out[:, cols] = both
+
+    def finish(at):
+        cols = pl.ds(*pieces[at])
+        total = g_out[:, cols]
+        for k in range(1, chips):
+            sums[at, k].wait_recv()
+            total = total + g_got[k - 1, :, cols].astype(f32)
+        if at == 0:
+            gi_ref[...] = total
+        elif at == 1:
+            gu_ref[...] = total
+        else:
+            go_ref[...] = total[:, :out_width].T
+            gd_ref[...] = total[:, out_width:].T
 
     for j in range((out_width + up_width) // wide):
         cols = slice(j * wide, (j + 1) * wide)
@@ -307,21 +346,20 @@
             p_grad = mul(m_grad, v_s[h, :seen, :], 1, 1)
             row_dot = jnp.sum(part * p_grad, axis=-1, keepdims=True)
             s_grad = (part * (p_grad - row_dot)).astype(bf16)
-            dq_s[h, at, :] = mul(s_grad, k_s[h, :seen, :], 1, 0) * scale
+            dq_s[h % 2, at, :] = mul(s_grad, k_s[h, :seen, :], 1, 0) * scale
             low_p[at, :seen] = part.astype(bf16)
             low_ds[at, :seen] = s_grad
         for b in range(tok_len // step_rows):
             at, late = slice(b * step_rows, (b + 1) * step_rows), slice(b * step_rows, tok_len)
-            dk_s[h, at, :] = mul(low_ds[late, at], q_s[h, late, :], 0, 0) * scale
-            dv_s[h, at, :] = mul(low_p[late, at], mg_s[h, late, :], 0, 0)
-
-    for h in range(heads):
-        attend_back(h)
+            dk_s[h % 2, at, :] = mul(low_ds[late, at], q_s[h, late, :], 0, 0) * scale
+            dv_s[h % 2, at, :] = mul(low_p[late, at], mg_s[h, late, :], 0, 0)
+
     in_sums = []
     for two in range(heads // 2):
         joined = []
-        for h in (two * 2, two * 2 + 1):
-            joined += [dq_s[h], dk_s[h], dv_s[h]]
+        for j in range(2):
+            attend_back(two * 2 + j)
+            joined += [dq_s[j], dk_s[j], dv_s[j]]
         part = turn(jnp.concatenate(joined, axis=1), -1.0).astype(bf16)
         tg[:, two * pair : (two + 1) * pair] = part
         in_sums.append(jnp.sum(part.astype(f32), axis=0, keepdims=True))
@@ -334,7 +372,7 @@
         m_grad = mul(hid_grad[at, :], w_all[:, at_up:at_out], 1, 1)
         n_out[k] = (a_grad * norm_vec[0] + m_grad * norm_vec[2]).astype(bf16)
         if k > 0:
-            n_moves.append(send(n_out.at[k], n_got.at[k], z_send, z_recv, (4, k), along[k]))
+            n_moves.append(send(n_out.at[k], n_got.at[k - 1], z_send, z_recv, (4, k), along[k]))
         part = normed[at, :]
         terms = [a_grad * part, a_grad, m_grad * part, m_grad]
         terms = [jnp.sum(term, axis=0, keepdims=True) for term in terms]
@@ -363,6 +401,7 @@
         for k in range(chips)
     ]
     add(0)
+    finish(2)
     v_across = []
     for k in order:
         v_give[k].wait_recv()
@@ -376,7 +415,7 @@
     own = x_ref[...].astype(f32)
     total = p_out[0].astype(f32)
     for k in range(1, groups):
-        total = total + p_got[k].astype(f32)
+        total = total + p_got[k - 1].astype(f32)
     lay_ref[...] = (own + total + out_bias).astype(bf16)
 
     total = v_sum[0]
@@ -390,12 +429,14 @@
         for k in range(1, groups)
     ]
 
+    finish(1)
+
     for copy in n_moves:
         copy.wait_recv()
     own_normed, own_std = normalise(own)
     total = n_out[0].astype(f32)
     for k in range(1, groups):
-        total = total + n_got[k].astype(f32)
+        total = total + n_got[k - 1].astype(f32)
     term = own_std * (
         total
         - jnp.mean(total, axis=-1, keepdims=True)
@@ -410,63 +451,63 @@
         total = total + v_last[k]
     v_out[...] = total
 
-    for copy in sums:
-        copy.wait_recv()
-    total = g_out[...]
-    for k in range(1, chips):
-        total = total + g_got[k].astype(f32)
-    g_out[...] = total
+    finish(0)
+    for way in range(2):
+        for j in range(groups - 1):
+            @pl.when(holds(way, j) & ways[way][2])
+            def _():
+                row_copy(way, j).wait_send()
     for copy in started:
         copy.wait_send()
 
 
-def layer(w, x, c, s, tables, chips, groups):
+def layer(weights, x, c, smalls, tables, chips, groups):
     vm = pl.BlockSpec(memory_space=pltpu.VMEM)
     dma = pltpu.SemaphoreType.DMA
-    length, depth, width = x.shape[0], w.shape[0], w.shape[1]
+    length, depth, width = x.shape[0], weights[0].shape[0], (4 * D + 2 * FF) // groups
     tok_len, devices, heads = length * groups, 2 * chips, H // groups
     up_width, in_width = FF // groups, 3 * D // groups
     shape, rows, head = (tok_len, D), (groups, length, D), (heads, tok_len, HD)
-    tile = (8, LANES)
+    late, two_heads, tile = (groups - 1, length, D), (2, tok_len, HD), (8, LANES)
     buffers = [
         ((D, width), bf16), (shape, bf16), (shape, bf16), ((devices, groups) + tile, f32),
         (shape, f32), (shape, bf16), (shape, bf16),
         ((D, tok_len), bf16), ((D, tok_len), bf16), ((D, tok_len), bf16),
-        (head, bf16), (head, bf16), (head, bf16), ((heads, tok_len, tok_len), f32), (head, f32),
+        (head, bf16), (head, bf16), (head, bf16), ((heads, tok_len, tok_len), f32), (head, bf16),
         ((tok_len, heads * HD + up_width), bf16), ((tok_len, up_width), f32),
-        ((tok_len, up_width), bf16), (head, bf16), (head, f32), (head, f32), (head, f32),
+        ((tok_len, up_width), bf16), (head, bf16), (two_heads, f32), (two_heads, f32), (two_heads, f32),
         ((tok_len, tok_len), bf16), ((tok_len, tok_len), bf16),
         ((tok_len, in_width), bf16),
-        (rows, bf16), (rows, bf16), (rows, bf16), (rows, bf16),
-        ((D, width), bf16), ((chips, depth, width), bf16), ((chips, depth, width), bf16),
-        ((chips, depth, width), bf16),
+        (rows, bf16), (late, bf16), (rows, bf16), (late, bf16),
+        ((D, width), bf16), ((chips, depth, width), bf16), ((chips - 1, depth, width), bf16),
+        ((chips - 1, depth, width), bf16),
         ((devices, groups) + tile, f32), ((chips, groups) + tile, f32), ((chips, groups) + tile, f32),
         ((chips, groups) + tile, f32), ((groups,) + tile, f32), ((groups,) + tile, f32),
+        ((depth, width), f32), (tile, f32),
     ]
-    sems = [(4,)] + [(3, chips)] * 4 + [(2, chips)] * 2 + [(6, groups)] * 2 + [(3, chips)] * 4 + [(2, chips)] * 2
+    sems = [(3, chips)] * 4 + [(2, chips)] * 2 + [(6, groups)] * 2 + [(2, groups)] * 2 + [(3, chips)] * 4 + [(2, chips)] * 2
     return pl.pallas_call(
         functools.partial(layer_kernel, chips, groups),
         out_shape=(
             jax.ShapeDtypeStruct(x.shape, bf16),
             jax.ShapeDtypeStruct(x.shape, bf16),
-            jax.ShapeDtypeStruct(w.shape, f32),
+            *[jax.ShapeDtypeStruct(weight.shape, f32) for weight in weights],
             jax.ShapeDtypeStruct(tile, f32),
         ),
-        in_specs=[vm] * 7,
-        out_specs=(vm,) * 4,
+        in_specs=[vm] * 11,
+        out_specs=(vm,) * 7,
         scratch_shapes=[pltpu.VMEM(*buffer) for buffer in buffers] + [dma(sem) for sem in sems],
         compiler_params=pltpu.CompilerParams(
             collective_id=0, has_side_effects=True, vmem_limit_bytes=60 * 2**20
         ),
         name="layer",
-    )(w, x, c, s, *tables)
+    )(*weights, x, c, *smalls, *tables)
 
 
 def body(hidden_in, out_grad, norm_params, biases, attn_in, attn_out, mlp_up, mlp_down):
     groups, devices = lax.axis_size("seq"), lax.axis_size("dp")
     chips = devices // 2
     length = hidden_in.shape[1]
-    in_width, out_width, up_width = attn_in.shape[1], attn_out.shape[0], mlp_up.shape[1]
     norm_size, bias_size = norm_params.shape[0], biases.shape[0]
     flat = lax.axis_index("dp") * groups + lax.axis_index("seq")
 
@@ -482,23 +523,26 @@
             return rows.reshape(size)
         return lax.dynamic_slice(rows.reshape(LANES), (flat % (LANES // size) * size,), (size,))
 
-    small = jnp.concatenate([tile_rows(norm_params.astype(f32)), tile_rows(biases.astype(f32))], axis=0)
-    norm_lines, lines = max(norm_size // LANES, 1), small.shape[0]
-    small = jnp.pad(small, ((0, 8 - lines), (0, 0)))
-    packed = jnp.concatenate([attn_in, mlp_up, attn_out.T, mlp_down.T], axis=1)
-    layer_out, grad_input, grads, sums = layer(
-        packed, hidden_in[0], out_grad[0], small, rotary_tables(length * groups), chips, groups
+    smalls = (tile_rows(norm_params), tile_rows(biases))
+    norm_lines, bias_lines = smalls[0].shape[0], smalls[1].shape[0]
+    layer_out, grad_input, grad_in, grad_out, grad_up, grad_down, sums = layer(
+        (attn_in, attn_out, mlp_up, mlp_down),
+        hidden_in[0],
+        out_grad[0],
+        smalls,
+        rotary_tables(length * groups),
+        chips,
+        groups,
     )
-    at_out = in_width + up_width
     return (
         layer_out[None],
         grad_input[None],
         from_rows(sums[:norm_lines], norm_size),
-        from_rows(sums[norm_lines:lines], bias_size),
-        grads[:, :in_width],
-        grads[:, at_out : at_out + out_width].T,
-        grads[:, in_width:at_out],
-        grads[:, at_out + out_width :].T,
+        from_rows(sums[norm_lines : norm_lines + bias_lines], bias_size),
+        grad_in,
+        grad_out,
+        grad_up,
+        grad_down,
     )
 
 

time: 129 us -> 122 us (0.946)
  local copies, waits for them, and re-layouts: 12.4 us -> 8.93 us
  other arithmetic: 3.26 us -> 0 us
    transpose x2 -> x0, local copies, waits for them, and re-layouts: 3.06 us -> none  [the longest x1 2.14 us: body(): grads[:, at_out + out_width:]]
    concatenate x1 -> x0, other arithmetic: 1.99 us -> none  [body(): packed = jnp.concatenate([attn_in, mlp_up, attn_out.T, mlp_down.T], axis=1)]
    slice x1 -> x0, local copies, waits for them, and re-layouts: 1.77 us -> none  [body(): grads[:, :in_width]]
    unnamed x10 -> x16, local copies, waits for them, and re-layouts: 5.19 us -> 6.48 us
where the time goes in v3:
time: 122 us
  Pallas kernels  112 us (92%)
  local copies, waits for them, and re-layouts  8.93 us (7%)
    pallas_call x1, Pallas kernels, layer(): pl.pallas_call(functools.partial(layer_kernel, chips, groups), out_shape=...  112 us
    unnamed x16, local copies, waits for them, and re-layouts  6.48 us
    reshape x2, local copies, waits for them, and re-layouts, from_rows(): return rows.reshape(size)  2.45 us

profile of v3, /device:TPU:0, one launch (start us, length us, event | category | flops | bytes accessed | tf_op | source)
XLA Modules:
  0.0 121.8 jit_solution(4888744013142392815)
XLA Ops:
  0.6 112.2 %layer.1 = (bf16[128,1024]{1,0:T(8,128)(2,1)}, bf16[128,1024]{1,0:T(8,128)(2,1)}, f32[128,768]{1,0:T(8,128)}, f32[256,128]{1,0:T(8,128)}, f32[128,1024]{1,0:T(8,...) custom-call(bf16[128,768]{1,0:T(8,128)(2,1)} %win_ref.1, bf16[256,128]{1,0:T(8,128)(2,1)} %wout_ref.1, ...), custom_call_target="tpu_custom_call" | custom-call | tf_op jit(solution)/shard_map/layer/pallas_call | solution.py:489
  112.9 1.2 slice_bitcast_fusion.1
  114.1 1.2 %slice_bitcast_fusion = f32[256]{0:T(256)} fusion(f32[8,128]{1,0:T(8,128)} %get-tuple-element.17), kind=kLoop, calls=%fused_computation | loop fusion | bytes 2048 | tf_op jit(solution)/shard_map/reshape | solution.py:523
  115.3 0.0 copy-start.3
  115.3 1.7 %copy.25 = bf16[1,128,1024]{2,1,0:T(8,128)(2,1)} copy(bf16[1,128,1024]{2,1,0:T(8,128)(2,1)} %bitcast.11) | data formatting | bytes 524288
  117.1 0.0 copy-done.3
  117.1 0.0 copy-start.2
  117.1 0.7 copy.26
  117.8 0.4 copy-done.2
  118.1 0.0 copy-start.4
  118.1 0.0 copy-start.1
  118.2 0.7 copy.27
  118.9 0.2 copy-done.4
  119.1 0.7 copy.28
  119.8 0.0 copy-done.1
  119.8 0.0 copy-start
  119.8 0.8 copy.29
  120.6 0.4 copy-done
  121.0 0.8 copy.30
Async XLA Ops:
  115.3 1.7 %copy-start.3 = (bf16[128,1024]{1,0:T(8,128)(2,1)S(1)}, bf16[128,1024]{1,0:T(8,128)(2,1)}, u32[]{:S(2)}) copy-start(bf16[128,1024]{1,0:T(8,128)(2,1)} %get-tuple-element.16) | copy-start | bytes 786436
  117.1 1.1 copy-start.2
  118.1 1.0 copy-start.4
  118.1 1.7 %copy-start.1 = (f32[128,1024]{1,0:T(8,128)S(1)}, f32[128,1024]{1,0:T(8,128)}, u32[]{:S(2)}) copy-start(f32[128,1024]{1,0:T(8,128)} %get-tuple-element.36) | copy-start | bytes 1572868
  119.8 1.2 %copy-start = (f32[1024,128]{1,0:T(8,128)S(1)}, f32[1024,128]{1,0:T(8,128)}, u32[]{:S(2)}) copy-start(f32[1024,128]{1,0:T(8,128)} %get-tuple-element.37) | copy-start | bytes 1572868

commit v4 on v3

--- a/solution.py
+++ b/solution.py
@@ -45,7 +45,7 @@
 def layer_kernel(
     chips, groups,
     win_ref, wout_ref, wup_ref, wdown_ref, x_ref, c_ref, nrm_ref, bias_ref, keep_ref, right_ref, left_ref,
-    lay_ref, gin_ref, gi_ref, go_ref, gu_ref, gd_ref, v_out,
+    lay_ref, gin_ref, gi_ref, go_ref, gu_ref, gd_ref, vn_out, vb_out,
     w_all, x_all, c_all, s_all, normed, rows_a, rows_m, turned_a, turned_m, turned_c,
     q_s, k_s, v_s, probs, mixed_s, both_rows, slope, hid_grad, mg_s, dq_s, dk_s, dv_s, low_p, low_ds, tg,
     p_out, p_got, n_out, n_got, g, g_half, g_sum, g_got, v_mine, v_half, v_sum, v_got, v_all, v_last,
@@ -329,15 +329,10 @@
         hid_grad[:, cols] = part
         up_sums.append(jnp.sum(part.astype(f32), axis=0, keepdims=True))
     add(2)
-    for j in range(up_width // wide):
-        cols = slice(j * wide, (j + 1) * wide)
-        g[:, at_up + j * wide : at_up + (j + 1) * wide] = mul(turned_m[...], hid_grad[:, cols], 1, 0).astype(bf16)
-    give(1)
 
     mixed_grad = mul(c_all[...], w_all[:, at_out:at_down], 1, 0).astype(bf16)
     for h in range(heads):
         mg_s[h] = mixed_grad[:, h * HD : (h + 1) * HD]
-    add(1)
 
     def attend_back(h):
         for b in range(tok_len // step_rows):
@@ -378,10 +373,15 @@
         terms = [jnp.sum(term, axis=0, keepdims=True) for term in terms]
         norm_sums = terms if norm_sums is None else [a + b for a, b in zip(norm_sums, terms)]
 
+    for j in range(up_width // wide):
+        cols = slice(j * wide, (j + 1) * wide)
+        g[:, at_up + j * wide : at_up + (j + 1) * wide] = mul(turned_m[...], hid_grad[:, cols], 1, 0).astype(bf16)
+    give(1)
     for j in range(in_width // wide):
         cols = slice(j * wide, (j + 1) * wide)
         g[:, cols] = mul(turned_a[...], tg[:, cols], 1, 0).astype(bf16)
     give(0)
+    add(1)
 
     v_mine[...] = jnp.zeros_like(v_mine)
 
@@ -449,7 +449,9 @@
     total = v_all[z]
     for k in range(1, groups):
         total = total + v_last[k]
-    v_out[...] = total
+    norm_lines = nrm_ref.shape[0]
+    vn_out[...] = total[:norm_lines]
+    vb_out[...] = total[norm_lines : norm_lines + bias_ref.shape[0]]
 
     finish(0)
     for way in range(2):
@@ -492,10 +494,10 @@
             jax.ShapeDtypeStruct(x.shape, bf16),
             jax.ShapeDtypeStruct(x.shape, bf16),
             *[jax.ShapeDtypeStruct(weight.shape, f32) for weight in weights],
-            jax.ShapeDtypeStruct(tile, f32),
+            *[jax.ShapeDtypeStruct(small.shape, f32) for small in smalls],
         ),
         in_specs=[vm] * 11,
-        out_specs=(vm,) * 7,
+        out_specs=(vm,) * 8,
         scratch_shapes=[pltpu.VMEM(*buffer) for buffer in buffers] + [dma(sem) for sem in sems],
         compiler_params=pltpu.CompilerParams(
             collective_id=0, has_side_effects=True, vmem_limit_bytes=60 * 2**20
@@ -524,8 +526,7 @@
         return lax.dynamic_slice(rows.reshape(LANES), (flat % (LANES // size) * size,), (size,))
 
     smalls = (tile_rows(norm_params), tile_rows(biases))
-    norm_lines, bias_lines = smalls[0].shape[0], smalls[1].shape[0]
-    layer_out, grad_input, grad_in, grad_out, grad_up, grad_down, sums = layer(
+    layer_out, grad_input, grad_in, grad_out, grad_up, grad_down, norm_sums, bias_sums = layer(
         (attn_in, attn_out, mlp_up, mlp_down),
         hidden_in[0],
         out_grad[0],
@@ -537,8 +538,8 @@
     return (
         layer_out[None],
         grad_input[None],
-        from_rows(sums[:norm_lines], norm_size),
-        from_rows(sums[norm_lines : norm_lines + bias_lines], bias_size),
+        from_rows(norm_sums, norm_size),
+        from_rows(bias_sums, bias_size),
         grad_in,
         grad_out,
         grad_up,

time: 122 us -> 122 us (level)
  Pallas kernels: 112 us -> 114 us
  local copies, waits for them, and re-layouts: 8.93 us -> 7.35 us
    reshape x2 -> x0, local copies, waits for them, and re-layouts: 2.45 us -> none  [from_rows(): return rows.reshape(size)]
    pallas_call x1, Pallas kernels: 112 us -> 114 us  [layer(): pl.pallas_call(functools.partial(layer_kernel, chips, groups), out_shape=...]
    unnamed x16 -> x22, local copies, waits for them, and re-layouts: 6.48 us -> 7.35 us
where the time goes in v4:
time: 122 us
  Pallas kernels  114 us (93%)
  local copies, waits for them, and re-layouts  7.35 us (6%)
    pallas_call x1, Pallas kernels, layer(): pl.pallas_call(functools.partial(layer_kernel, chips, groups), out_shape=...  114 us
    unnamed x22, local copies, waits for them, and re-layouts  7.35 us

profile of v4, /device:TPU:0, one launch (start us, length us, event | category | flops | bytes accessed | tf_op | source)
XLA Modules:
  0.0 122.1 jit_solution(7302437279509828102)
XLA Ops:
  0.6 114.1 %layer.1 = (bf16[128,1024]{1,0:T(8,128)(2,1)}, bf16[128,1024]{1,0:T(8,128)(2,1)}, f32[128,768]{1,0:T(8,128)}, f32[256,128]{1,0:T(8,128)}, f32[128,1024]{1,0:T(8,...) custom-call(bf16[128,768]{1,0:T(8,128)(2,1)} %win_ref.1, bf16[256,128]{1,0:T(8,128)(2,1)} %wout_ref.1, ...), custom_call_target="tpu_custom_call" | custom-call | tf_op jit(solution)/shard_map/layer/pallas_call | solution.py:491
  114.8 0.0 copy-start.3
  114.8 1.7 %copy.27 = bf16[1,128,1024]{2,1,0:T(8,128)(2,1)} copy(bf16[1,128,1024]{2,1,0:T(8,128)(2,1)} %bitcast.9) | data formatting | bytes 524288
  116.5 0.0 copy-done.3
  116.5 0.0 copy-start.6
  116.5 0.0 copy-start.2
  116.5 0.7 copy.28
  117.2 0.0 copy-done.6
  117.2 0.0 copy-start.5
  117.2 0.5 copy.29
  117.7 0.2 copy-done.5
  117.9 0.6 copy.30
  118.5 0.0 copy-done.2
  118.5 0.0 copy-start.4
  118.5 0.0 copy-start.1
  118.5 0.7 copy.31
  119.2 0.2 copy-done.4
  119.5 0.7 copy.32
  120.1 0.0 copy-done.1
  120.1 0.0 copy-start
  120.1 0.8 copy.33
  120.9 0.4 copy-done
  121.3 0.8 copy.34
Async XLA Ops:
  114.8 1.7 %copy-start.3 = (bf16[128,1024]{1,0:T(8,128)(2,1)S(1)}, bf16[128,1024]{1,0:T(8,128)(2,1)}, u32[]{:S(2)}) copy-start(bf16[128,1024]{1,0:T(8,128)(2,1)} %get-tuple-element.17) | copy-start | bytes 786436
  116.5 0.7 copy-start.6
  116.5 2.0 %copy-start.2 = (f32[128,768]{1,0:T(8,128)S(1)}, f32[128,768]{1,0:T(8,128)}, u32[]{:S(2)}) copy-start(f32[128,768]{1,0:T(8,128)} %get-tuple-element.36) | copy-start | bytes 1179652
  117.2 0.7 copy-start.5
  118.5 1.0 copy-start.4
  118.5 1.7 %copy-start.1 = (f32[128,1024]{1,0:T(8,128)S(1)}, f32[128,1024]{1,0:T(8,128)}, u32[]{:S(2)}) copy-start(f32[128,1024]{1,0:T(8,128)} %get-tuple-element.38) | copy-start | bytes 1572868
  120.1 1.2 %copy-start = (f32[1024,128]{1,0:T(8,128)S(1)}, f32[1024,128]{1,0:T(8,128)}, u32[]{:S(2)}) copy-start(f32[1024,128]{1,0:T(8,128)} %get-tuple-element.39) | copy-start | bytes 1572868
